TPU v7x, 512 devices: a whole 4x8x8 slice. The times are simulated.
512 devices in a mesh: row: 64 (over y, z), col: 8 (over x, core).
Axes of the slice: x: 4, y: 8, z: 8, core: 2. Of those that a mesh axis runs over, the one named last changes fastest.
Arguments:
- tokens: bfloat16 [2048, 6144], P(('row', 'col')), may hold values from -6 to 6
- norm_gain: float32 [6144], replicated, may hold values from 0.1 to 1.9
- in_weight: bfloat16 [6144, 24576], P('row', 'col'), may hold values from -0.078125 to 0.078125
- out_weight: bfloat16 [24576, 6144], P('row', 'col'), may hold values from -0.0390625 to 0.0390625
Outputs:
- block_out: bfloat16 [2048, 6144], P(('row', 'col'))
All inputs are finite; a program needn't handle non-finite values.
Results may differ from a plain program's by a relative error of at most 0.0042.
Values may be sent and summed in bfloat16 or wider, within the bound.
A program may use at most 64 MiB of HBM per device.

v0:
```python
import jax
import jax.numpy as jnp
from jax import lax
from jax.sharding import PartitionSpec as P


def normalize(rows, norm_gain):
    values = rows.astype(jnp.float32)
    center = jnp.mean(values, axis=1, keepdims=True)
    spread = jnp.mean(jnp.square(values - center), axis=1, keepdims=True)
    scaled = (values - center) / jnp.sqrt(spread + 1e-06) * norm_gain
    return scaled.astype(jnp.bfloat16)


def add_sources(received):
    return jnp.sum(received, axis=0)


def body(tokens, norm_gain, in_weight, out_weight):
    row_count = lax.axis_size("row")
    col_count = lax.axis_size("col")
    per_panel = row_count // col_count
    slice_width = out_weight.shape[0] // row_count
    in_parts = in_weight.reshape(in_weight.shape[0], per_panel, row_count, slice_width)
    out_parts = out_weight.reshape(1, 1, row_count, slice_width * out_weight.shape[1])
    in_moved, out_moved = (
        lax.all_to_all(in_parts, "row", split_axis=2, concat_axis=0, tiled=True),
        lax.all_to_all(out_parts, "row", split_axis=2, concat_axis=0, tiled=True),
    )
    in_cols = in_moved.reshape(in_moved.shape[0], per_panel * slice_width)
    out_rows = out_moved.reshape(row_count * slice_width, out_weight.shape[1])
    in_panel, out_panel = (
        lax.all_gather(in_cols, "col", axis=1, tiled=True),
        lax.all_gather(out_rows, "col", axis=1, tiled=True),
    )
    gathered = lax.all_gather(tokens, "row", axis=0, tiled=True)
    normed = normalize(gathered, norm_gain)
    pre = jnp.dot(normed, in_panel, preferred_element_type=jnp.float32)
    hidden = jax.nn.gelu(pre, approximate=True).astype(jnp.bfloat16)
    terms = jnp.dot(hidden, out_panel, preferred_element_type=jnp.float32)
    blocks = terms.reshape(row_count, tokens.shape[0], terms.shape[1])
    summed = add_sources(lax.all_to_all(blocks, "row", split_axis=0, concat_axis=0, tiled=True))
    return (tokens.astype(jnp.float32) + summed).astype(jnp.bfloat16)


def solution(mesh):
    return jax.shard_map(
        body,
        mesh=mesh,
        in_specs=(P(("row", "col"), None), P(), P("row", "col"), P("row", "col")),
        out_specs=P(("row", "col"), None),
        check_vma=False,
    )
```

profile of v0, /device:TPU:32, one launch (start us, length us, event | category | flops | bytes accessed | tf_op | source)
XLA Modules:
  0.0 406.7 jit_solution(15552510265398028493)
XLA Ops:
  6.5 0.7 all-gather.9.cloned.1.call-update
  7.3 1.4 copy.10
  8.7 0.3 reshape.33
  9.1 0.9 copy.11
  10.0 38.7 %all_to_all.29 = bf16[96,8,64,6]{0,1,3,2:T(8,128)(2,1)S(1)} all-to-all(bf16[96,8,64,6]{0,1,3,2:T(8,128)(2,1)S(1)} %copy.11), channel_id=1, replica_groups=mesh['row'=64,'col'=8] {'row'}, dimensions={2} | all-to-all | bytes 1179648 | tf_op jit(solution)/shard_map/all_to_all | solution.py:27
  48.9 1.9 reshape.34
  50.9 0.3 reshape.44
  51.2 0.5 broadcast.27
  51.7 4.2 %reduce.4 = bf16[64,4608]{1,0:T(8,128)(2,1)S(1)} reduce(bf16[64,1,1,4608]{3,2,1,0:T(2,128)(2,1)S(1)} %bitcast.15, bf16[]{:T(256)} %broadcast.27), dimensions={1,2}, to_apply=%bitcast.10.reduce_sub_computation | reduce | bytes 1179650
  56.0 25.8 %all_to_all.30 = bf16[64,2,2304]{2,1,0:T(2,128)(2,1)S(1)} all-to-all(bf16[64,2,2304]{2,1,0:T(2,128)(2,1)S(1)} %reshape.46), channel_id=1, replica_groups=mesh['row'=64,'col'=8] {'row'}, dimensions={0} | all-to-all | bytes 1179648 | tf_op jit(solution)/shard_map/all_to_all | solution.py:28
  81.8 0.5 reshape.47
  82.3 3.4 bitcast_reduce_fusion
  85.7 1.4 reshape.36
  87.1 21.4 %all-gather.9.cloned.1.call-done = bf16[64,4,6144]{2,1,0:T(4,128)(2,1)} async-done(((bf16[1,4,6144]{2,1,0:T(4,128)(2,1)}), bf16[64,4,6144]{2,1,0:T(4,128)(2,1)}) %all-gather.9.cloned.1.call-update) | async-done | bytes 3145744 | tf_op jit(solution)/shard_map/all_gather | solution.py:36
  108.5 3.2 convert_reduce_fusion
  111.8 6.2 %reshape.40 = f32[256,6144]{1,0:T(8,128)} reshape(bf16[64,4,6144]{2,1,0:T(4,128)(2,1)} %all-gather.9.cloned.1.call-done) | data formatting | bytes 9437184 | tf_op jit(solution)/shard_map/convert_element_type | solution.py:8
  118.0 3.6 multiply_reduce_fusion
  121.6 26.8 %all-gather.5.cloned.1.call-done = bf16[6144,384]{0,1:T(8,128)(2,1)} async-done(((bf16[6144,48]{0,1:T(8,128)(2,1)}), bf16[6144,384]{0,1:T(8,128)(2,1)}) %all-gather.5.cloned.1.call-update) | async-done | bytes 4718608 | tf_op jit(solution)/shard_map/all_gather | solution.py:33
  148.4 41.8 %all-gather.7.cloned.1.call-done = bf16[384,6144]{1,0:T(8,128)(2,1)} async-done(((bf16[384,768]{1,0:T(8,128)(2,1)}), bf16[384,6144]{1,0:T(8,128)(2,1)}) %all-gather.7.cloned.1.call-update) | async-done | bytes 4718608 | tf_op jit(solution)/shard_map/all_gather | solution.py:34
  190.2 11.9 %fusion.9 = f32[256,6144]{1,0:T(8,128)} fusion(bf16[384,6144]{1,0:T(8,128)(2,1)} %all-gather.7.cloned.1.call-done, bf16[6144,384]{0,1:T(8,128)(2,1)} %all-gather.5.cloned.1.call-done, f32[256,6144]{1,0:T(8,128)} %reshape.40, f32[6144]{0:T(1024)S(1)} %copy-done.2, f32[256]{0:T(256)S(1)} %add_sqrt_fusion, f32[256]{0:T(256)S(1)} %reshape.43), kind=kOutput, calls=%fused_computation.13 | convolution fusion | flops 2423095296 | bytes 22046720 | tf_op jit(solution)/shard_map/dot_general | solution.py:40
  202.1 7.8 %reshape.37 = f32[64,4,6144]{2,1,0:T(4,128)} reshape(f32[256,6144]{1,0:T(8,128)} %fusion.9) | data formatting | bytes 12582912 | tf_op jit(solution)/shard_map/reshape | solution.py:41
  209.9 185.8 %all_to_all.31 = f32[64,4,6144]{2,1,0:T(4,128)} all-to-all(f32[64,4,6144]{2,1,0:T(4,128)} %reshape.37), channel_id=1, replica_groups=mesh['row'=64,'col'=8] {'row'}, dimensions={0} | all-to-all | bytes 12582912 | tf_op jit(solution)/shard_map/all_to_all | solution.py:42
  395.7 3.8 reduce_sum.29
  399.5 0.6 add_convert_fusion
  (16 shorter events, 0.6 us)
Async XLA Ops:
  6.5 44.3 %copy-start = (bf16[384,768]{1,0:T(8,128)(2,1)S(1)}, bf16[384,768]{1,0:T(8,128)(2,1)}, u32[]{:S(2)}) copy-start(bf16[384,768]{1,0:T(8,128)(2,1)} %param.7) | copy-start | bytes 1769476
  6.5 101.9 %all-gather.9.cloned.1.call-start = ((), (), s32[]{:S(2)}) async-start(), calls=%async_computation.5 | async-start | bytes 3194880 | tf_op jit(solution)/shard_map/all_gather | solution.py:36
  7.3 141.1 %all-gather.5.cloned.1.call-start = ((), (), s32[]{:S(2)}) async-start(), calls=%async_computation.3 | async-start | bytes 5308416 | tf_op jit(solution)/shard_map/all_gather | solution.py:33
  50.8 139.4 %all-gather.7.cloned.1.call-start = ((), (), s32[]{:S(2)}) async-start(), calls=%async_computation.4 | async-start | bytes 5308416 | tf_op jit(solution)/shard_map/all_gather | solution.py:34
  111.8 78.4 %copy-start.2 = (f32[6144]{0:T(1024)S(1)}, f32[6144]{0:T(1024)}, u32[]{:S(2)}) copy-start(f32[6144]{0:T(1024)} %param.5) | copy-start | bytes 73732
  395.7 3.8 copy-start.1
Sparse Core Ops, SparseCore 0:
  10.4 97.9 all-gather.8
  110.6 37.7 all-gather.4
  150.5 39.6 all-gather.6
where the time goes:
time: 407 us
  blocking collectives  250 us (61%)
  waiting for transfers between devices  90.7 us (22%)
  local copies, waits for them, and re-layouts  25.1 us (6%)
  other arithmetic  15.4 us (4%)
  between operations  13.2 us (3%)
  matrix products  11.9 us (3%)
    all_to_all x1, blocking collectives, body(): lax.all_to_all(blocks, 'row', split_axis=0, concat_axis=0, tiled=True)  186 us
    all_gather x1, waiting for transfers between devices, body(): lax.all_gather(out_rows, 'col', axis=1, tiled=True)  41.8 us
    all_to_all x1, blocking collectives, body(): lax.all_to_all(in_parts, 'row', split_axis=2, concat_axis=0, tiled=True)  38.7 us
    all_gather x1, waiting for transfers between devices, body(): lax.all_gather(in_cols, 'col', axis=1, tiled=True)  26.8 us
    all_to_all x1, blocking collectives, body(): lax.all_to_all(out_parts, 'row', split_axis=2, concat_axis=0, tiled=True)  25.8 us
    all_gather x1, waiting for transfers between devices, body(): gathered = lax.all_gather(tokens, 'row', axis=0, tiled=True)  21.4 us
    dot_general x1, matrix products, body(): terms = jnp.dot(hidden, out_panel, preferred_element_type=jnp.float32)  11.9 us
  transfers between devices with their start and end apart: 3, of which 3 were waited for; matrix products, arithmetic and copies ran while one was open for 7% of the time, Pallas kernels for 0%

commit v1 on v0

v1 whole, which is shorter than its diff:
```python
import jax
import jax.numpy as jnp
from jax import lax
from jax.experimental import pallas as pl
from jax.experimental.pallas import tpu as pltpu
from jax.sharding import PartitionSpec as P

MESH = pl.DeviceIdType.MESH
N = 8
BF16 = jnp.bfloat16
F32 = jnp.float32


def gelu(v):
    return 0.5 * v * (1.0 + jnp.tanh(0.7978845608028654 * (v + 0.044715 * (v * v * v))))


def rows_of(block):
    return block.reshape(block.shape[0] * block.shape[1], block.shape[2])


def kernel(
    tok_ref, gain_ref, inw_ref, outw_ref, out_ref,
    w1, w2, norm_out, norm_in, slab, x_buf, hid_out, h_buf,
    ring_send, ring_recv, part, part_in, own_part, fin_out, fin_in,
    w_sem, y_send, y_recv, w_send, w_recv, z_send, z_recv,
    xg_near, xg_relay, xg_sib, xg_recv, hg_near, hg_relay, hg_sib, hg_recv,
    ha_send, ha_recv, rs_send, rs_recv, p_send, p_recv, f_send, f_recv,
):
    row, c = lax.axis_index("row"), lax.axis_index("col")
    y, z = row // N, row % N
    x, core = c // 2, c % 2

    def dev(y_at, z_at, c_at):
        return (y_at * N + z_at, c_at)

    def col_of(x_at, core_at):
        return ((x_at + 8) % 4) * 2 + core_at

    def remote(src, dst, send, recv, target):
        return pltpu.make_async_remote_copy(
            src_ref=src, dst_ref=dst, send_sem=send, recv_sem=recv, device_id=target, device_id_type=MESH
        )

    right, left, across, sibling = col_of(x + 1, core), col_of(x - 1, core), col_of(x + 2, core), col_of(x, 1 - core)

    barrier = pltpu.get_barrier_semaphore()

    def greet(target):
        pl.semaphore_signal(barrier, inc=1, device_id=target, device_id_type=MESH)

    def greet_line(k, _):
        greet(dev((y + k) % N, z, c))
        greet(dev(y, (z + k) % N, c))
        return 0

    lax.fori_loop(1, N, greet_line, 0)
    for target in (right, left, sibling):
        greet(dev(y, z, target))

    def greet_plane(p, _):
        @pl.when(jnp.logical_or(y != c, p != c))
        def _():
            greet(dev(c, z, p))
            greet(dev(p, z, y))

        return 0

    lax.fori_loop(0, N, greet_plane, 0)

    own_w1 = pltpu.make_async_copy(inw_ref.at[:, pl.ds(pl.multiple_of(z * 384, 384), 384)], w1.at[z], w_sem.at[0])
    own_w1.start()
    own_w2 = [
        pltpu.make_async_copy(outw_ref.at[:, pl.ds(384 * j, 384)], w2.at[j], w_sem.at[1 + j]) for j in range(2)
    ]
    for copy in own_w2:
        copy.start()

    values = tok_ref[...].astype(F32)
    center = jnp.mean(values, axis=1, keepdims=True)
    spread = jnp.mean(jnp.square(values - center), axis=1, keepdims=True)
    normed = ((values - center) / jnp.sqrt(spread + 1e-06) * gain_ref[...]).astype(BF16)
    for j in range(N):
        norm_out[j] = normed[:, 768 * j : 768 * (j + 1)]
    norm_in[pl.ds(y, 1)] = norm_out[pl.ds(y, 1)]

    @pl.when(y == c)
    def _():
        pl.semaphore_wait(barrier, 31)

    @pl.when(y != c)
    def _():
        pl.semaphore_wait(barrier, 33)

    def y_copy(k):
        to = (y + k) % N
        return remote(norm_out.at[to], norm_in.at[y], y_send.at[k], y_recv.at[k], dev(to, z, c))

    def w_copy(k):
        to = (z + k) % N
        return remote(
            inw_ref.at[:, pl.ds(pl.multiple_of(to * 384, 384), 384)], w1.at[z], w_send.at[k], w_recv.at[k], dev(y, to, c)
        )

    def z_copy(k):
        to = (z + k) % N
        return remote(x_buf.at[c, z], x_buf.at[c, z], z_send.at[k], z_recv.at[k], dev(y, to, c))

    def over(start, make, act):
        def step(k, _):
            act(make(k))
            return 0

        lax.fori_loop(start, N, step, 0)

    over(1, y_copy, lambda copy: copy.start())
    over(1, w_copy, lambda copy: copy.start())
    over(1, y_copy, lambda copy: copy.wait_recv())
    for j in range(N):
        slab[4 * j : 4 * j + 4, 0:768] = norm_in[j].astype(F32)
    x_buf[c, z] = slab[:, 0:768].astype(BF16)
    over(1, z_copy, lambda copy: copy.start())

    def gather_cols(buf, ready, near, relay, sib, recv):
        def block(of, h):
            return buf.at[of, pl.ds(4 * h, 4)]

        def send(of, h, sem, target):
            copy = remote(block(of, h), block(of, h), sem, recv.at[of, h], dev(y, z, target))
            copy.start()
            return copy

        def arrived(of, h):
            remote(block(of, h), block(of, h), sib.at[0, 0], recv.at[of, h], dev(y, z, sibling)).wait_recv()

        sent = []
        for h in range(2):
            ready(h)
            sent.append(send(c, h, near.at[0, h], right))
            sent.append(send(c, h, near.at[1, h], left))
            sent.append(send(c, h, sib.at[0, h], sibling))
        arrived(left, 0)
        sent.append(send(left, 0, relay.at[0], right))
        arrived(right, 0)
        arrived(right, 1)
        sent.append(send(right, 1, relay.at[1], left))
        sent.append(send(left, 0, sib.at[1, 0], sibling))
        sent.append(send(right, 1, sib.at[2, 1], sibling))
        sent.append(send(right, 0, sib.at[2, 0], sibling))
        arrived(left, 1)
        sent.append(send(left, 1, sib.at[1, 1], sibling))
        for h in range(2):
            arrived(across, h)
            sent.append(send(across, h, sib.at[3, h], sibling))

        def rest():
            for d in range(4):
                for h in range(2):
                    arrived(col_of(x + d, 1 - core), h)

        return sent, rest

    def z_ready(h):
        def step(j, _):
            k = (z - j + N) % N

            @pl.when(k > 0)
            def _():
                z_copy(k).wait_recv()

            return 0

        lax.fori_loop(4 * h, 4 * h + 4, step, 0)

    sent_x, rest = gather_cols(x_buf, z_ready, xg_near, xg_relay, xg_sib, xg_recv)
    rest()
    own_w1.wait()
    over(1, w_copy, lambda copy: copy.wait_recv())

    def chain(q):
        h, back = q % 2, q // 2
        steps = 4 - (h + back) % 2
        return h, 1 - 2 * back, steps

    def ring_copy(at, q, s, place, neighbour):
        _, way, _ = chain(q)
        return remote(
            ring_send.at[at, q, s], ring_recv.at[at, q, s], rs_send.at[at, q, s], rs_recv.at[at, q, s],
            neighbour((place + way + N) % N),
        )

    def ring_step(at, q, s, place, neighbour, own):
        h, way, steps = chain(q)

        @pl.when(s < steps)
        def _():
            to = (place + way * (steps - s) + N) % N
            mine = own(to, h)

            @pl.when(s == 0)
            def _():
                ring_send[at, q, s] = mine.astype(BF16)

            @pl.when(s > 0)
            def _():
                before = jnp.maximum(s - 1, 0)
                ring_copy(at, q, before, place, neighbour).wait_recv()
                ring_send[at, q, s] = (mine + ring_recv[at, q, before].astype(F32)).astype(BF16)

            ring_copy(at, q, s, place, neighbour).start()

    def ring_last(at, h, place, neighbour, own):
        total = own(place, h)
        for q in (h, 2 + h):
            last = 3 - (h + q // 2) % 2
            ring_copy(at, q, last, place, neighbour).wait_recv()
            total = total + ring_recv[at, q, last].astype(F32)
        return total

    def rings(each):
        def step(i, _):
            for at, place, neighbour, own in each:
                ring_step(at, i % 4, i // 4, place, neighbour, own)
            return 0

        lax.fori_loop(0, 16, step, 0)

    def rings_sent(each):
        def step(i, _):
            for at, place, neighbour, own in each:
                q, s = i % 4, i // 4

                @pl.when(s < chain(q)[2])
                def _():
                    ring_copy(at, q, s, place, neighbour).wait_send()

            return 0

        lax.fori_loop(0, 16, step, 0)

    def along_y(to):
        return dev(to, z, c)

    def along_z(to):
        return dev(y, to, c)

    def pre_part(to, h):
        lhs = rows_of(x_buf[to, pl.ds(4 * h, 4)])
        return jnp.dot(lhs, rows_of(w1[...]), preferred_element_type=F32)

    ring_pre = (0, y, along_y, pre_part)
    rings([ring_pre])
    for h in range(2):
        hidden = gelu(ring_last(0, h, y, along_y, pre_part)).astype(BF16)
        hid_out[4 * h : 4 * h + 4] = hidden.reshape(4, 32, 384)

    def own_slot(p):
        return jnp.logical_and(y == c, p == c)

    def ha_copy(p):
        return remote(hid_out.at[p], h_buf.at[p, y], ha_send.at[p], ha_recv.at[y], dev(c, z, p))

    def ha_start(p, _):
        @pl.when(own_slot(p))
        def _():
            h_buf[p, y] = hid_out[p]

        @pl.when(jnp.logical_not(own_slot(p)))
        def _():
            ha_copy(p).start()

        return 0

    lax.fori_loop(0, N, ha_start, 0)

    def h_ready(h):
        def step(j, _):
            @pl.when(jnp.logical_or(y != c, j != c))
            def _():
                remote(hid_out.at[j], h_buf.at[c, j], ha_send.at[j], ha_recv.at[j], dev(j, z, y)).wait_recv()

            return 0

        lax.fori_loop(4 * h, 4 * h + 4, step, 0)

    sent_h, rest = gather_cols(h_buf, h_ready, hg_near, hg_relay, hg_sib, hg_recv)
    for copy in own_w2:
        copy.wait()
    rest()

    def out_part_a(to, h):
        return jnp.dot(rows_of(h_buf[pl.ds(4 * h, 4), to]), w2[0], preferred_element_type=F32)

    def out_part_b(to, h):
        return jnp.dot(rows_of(h_buf[to, pl.ds(4 * h, 4)]), w2[1], preferred_element_type=F32)

    ring_a, ring_b = (1, y, along_y, out_part_a), (2, z, along_z, out_part_b)
    rings([ring_a, ring_b])
    others = ((z, along_z), (y, along_y))

    def p_copy(j, k):
        place, neighbour = others[j]
        to = (place + k) % N
        return remote(part.at[j, to], part_in.at[j, place], p_send.at[j, k], p_recv.at[j, k], neighbour(to))

    for h in range(2):
        for j, (at, place, neighbour, own) in enumerate((ring_a, ring_b)):
            total = ring_last(at, h, place, neighbour, own).reshape(4, 32, 384)
            own_part[j, 4 * h : 4 * h + 4] = total
            part[j, 4 * h : 4 * h + 4] = total.astype(BF16)

    def p_start(k, _):
        for j in range(2):
            p_copy(j, k).start()
        return 0

    lax.fori_loop(1, N, p_start, 0)
    for j in range(2):
        place = others[j][0]

        def p_add(k, total):
            p_copy(j, k).wait_recv()
            return total + part_in[j, (place - k + N) % N].astype(F32)

        slab[:, 384 * j : 384 * (j + 1)] = lax.fori_loop(1, N, p_add, own_part[j, place])

    for j in range(N):
        fin_out[j] = slab[4 * j : 4 * j + 4, 0:768]

    def f_copy(p):
        return remote(fin_out.at[p], fin_in.at[c], f_send.at[p], f_recv.at[c], dev(p, z, y))

    def f_start(p, _):
        @pl.when(jnp.logical_and(y == c, p == y))
        def _():
            fin_in[c] = fin_out[p]

        @pl.when(jnp.logical_or(y != c, p != y))
        def _():
            f_copy(p).start()

        return 0

    lax.fori_loop(0, N, f_start, 0)

    over(1, y_copy, lambda copy: copy.wait_send())
    over(1, w_copy, lambda copy: copy.wait_send())
    over(1, z_copy, lambda copy: copy.wait_send())
    for copy in sent_x + sent_h:
        copy.wait_send()
    rings_sent([ring_pre, ring_a, ring_b])

    def p_sent(k, _):
        for j in range(2):
            p_copy(j, k).wait_send()
        return 0

    lax.fori_loop(1, N, p_sent, 0)

    def plane_sent(p, _):
        @pl.when(jnp.logical_or(y != c, p != c))
        def _():
            ha_copy(p).wait_send()
            f_copy(p).wait_send()
            remote(fin_out.at[p], fin_in.at[p], f_send.at[p], f_recv.at[p], dev(c, z, p)).wait_recv()

        return 0

    lax.fori_loop(0, N, plane_sent, 0)
    for j in range(N):
        cols = slice(768 * j, 768 * (j + 1))
        out_ref[:, cols] = (tok_ref[:, cols].astype(F32) + fin_in[j]).astype(BF16)


def body(tokens, norm_gain, in_weight, out_weight):
    dma = pltpu.SemaphoreType.DMA
    vmem = pl.BlockSpec(memory_space=pltpu.VMEM)
    return pl.pallas_call(
        kernel,
        out_shape=jax.ShapeDtypeStruct(tokens.shape, BF16),
        in_specs=[vmem, vmem, pl.BlockSpec(memory_space=pl.ANY), pl.BlockSpec(memory_space=pl.ANY)],
        out_specs=vmem,
        scratch_shapes=[
            pltpu.VMEM((N, 96, 384), BF16),
            pltpu.VMEM((2, 384, 384), BF16),
            pltpu.VMEM((N, 4, 768), BF16),
            pltpu.VMEM((N, 4, 768), BF16),
            pltpu.VMEM((32, 768), F32),
            pltpu.VMEM((N, N, 32, 768), BF16),
            pltpu.VMEM((N, 32, 384), BF16),
            pltpu.VMEM((N, N, 32, 384), BF16),
            pltpu.VMEM((3, 4, 4, 128, 384), BF16),
            pltpu.VMEM((3, 4, 4, 128, 384), BF16),
            pltpu.VMEM((2, N, 32, 384), BF16),
            pltpu.VMEM((2, N, 32, 384), BF16),
            pltpu.VMEM((2, N, 32, 384), F32),
            pltpu.VMEM((N, 4, 768), F32),
            pltpu.VMEM((N, 4, 768), F32),
            dma((3,)),
            dma((N,)), dma((N,)), dma((N,)), dma((N,)), dma((N,)), dma((N,)),
            dma((2, 2)), dma((2,)), dma((4, 2)), dma((N, 2)),
            dma((2, 2)), dma((2,)), dma((4, 2)), dma((N, 2)),
            dma((N,)), dma((N,)),
            dma((3, 4, 4)), dma((3, 4, 4)),
            dma((2, N)), dma((2, N)),
            dma((N,)), dma((N,)),
        ],
        compiler_params=pltpu.CompilerParams(
            collective_id=0, has_side_effects=True, vmem_limit_bytes=48 * 1024 * 1024
        ),
        cost_estimate=pl.CostEstimate(flops=2_500_000_000, bytes_accessed=1_300_000, transcendentals=100_000),
    )(tokens, norm_gain.reshape(1, -1), in_weight, out_weight)


def solution(mesh):
    return jax.shard_map(
        body,
        mesh=mesh,
        in_specs=(P(("row", "col"), None), P(), P("row", "col"), P("row", "col")),
        out_specs=P(("row", "col"), None),
        check_vma=False,
    )
```

time: 407 us -> 143 us (0.35)
  the two profiles are of different devices: /device:TPU:32 before, /device:TPU:1 now
where the time goes in v1:
time: 143 us
  Pallas kernels  139 us (97%)
  local copies, waits for them, and re-layouts  4.28 us (3%)
    pallas_call x1, Pallas kernels, body(): pl.pallas_call(kernel, out_shape=jax.ShapeDtypeStruct(tokens.shape, BF16)...  139 us
    unnamed x9, local copies, waits for them, and re-layouts  4.28 us

profile of v1, /device:TPU:1, one launch (start us, length us, event | category | flops | bytes accessed | tf_op | source)
XLA Modules:
  0.0 142.8 jit_solution(11953388290009571008)
XLA Ops:
  0.0 0.0 copy-start
  0.0 1.1 copy-done
  1.1 0.0 copy-start.1
  1.1 1.1 copy-done.1
  2.1 0.0 copy-start.2
  2.1 0.8 copy-done.2
  2.9 0.0 copy-start.3
  2.9 0.7 copy-done.3
  3.7 138.5 %shard_map.46 = bf16[4,6144]{1,0:T(4,128)(2,1)S(1)} custom-call(bf16[4,6144]{1,0:T(4,128)(2,1)S(1)} %copy-done.2, f32[1,6144]{1,0:T(1,128)S(1)} %bitcast.1, bf16[96,3072]{1,0:T(8,128)(2,1)S(1)} %copy-done, bf16[384,768]{1,0:T(8,128)(2,1)S(1)} %copy-done.1), custom_call_target="tpu_custom_call" | custom-call | flops 2500000000 | bytes 1300000 | tf_op jit(solution)/shard_map/pallas_call | solution.py:378
  142.2 0.6 copy.6
Async XLA Ops:
  0.0 1.1 copy-start
  1.1 1.1 copy-start.1
  2.1 0.8 copy-start.2
  2.9 0.7 copy-start.3

commit v2 on v1

v2 whole, which is shorter than its diff:
```python
import jax
import jax.numpy as jnp
from jax import lax
from jax.experimental import pallas as pl
from jax.experimental.pallas import tpu as pltpu
from jax.sharding import PartitionSpec as P

MESH = pl.DeviceIdType.MESH
N = 8
BF16 = jnp.bfloat16
F32 = jnp.float32


def gelu(v):
    return 0.5 * v * (1.0 + jnp.tanh(0.7978845608028654 * (v + 0.044715 * (v * v * v))))


def rows_of(block):
    return block.reshape(block.shape[0] * block.shape[1], block.shape[2])


def kernel(
    tok_hbm, gain_hbm, inw_ref, outw_ref, out_ref,
    tok_ref, gain_ref, w1, w2, norm_out, norm_in, slab, x_buf, hid_out, hid_in, h_buf,
    ring_send, ring_recv, part, part_in, own_part, fin_out, fin_in,
    w_sem, y_send, y_recv, w_send, w_recv, xz_send, xg_send, xg_recv, hg_send, hg_recv,
    hc_send, hc_recv, hy_send, rs_send, rs_recv, p_send, p_recv, f_send, f_recv,
):
    row, c = lax.axis_index("row"), lax.axis_index("col")
    y, z = row // N, row % N
    x, core = c // 2, c % 2

    def dev(y_at, z_at, c_at):
        return (y_at * N + z_at, c_at)

    def col_of(x_at, core_at):
        return ((x_at + 8) % 4) * 2 + core_at

    def remote(src, dst, send, recv, target):
        return pltpu.make_async_remote_copy(
            src_ref=src, dst_ref=dst, send_sem=send, recv_sem=recv, device_id=target, device_id_type=MESH
        )

    right, left, across, sibling = col_of(x + 1, core), col_of(x - 1, core), col_of(x + 2, core), col_of(x, 1 - core)

    barrier = pltpu.get_barrier_semaphore()

    def greet(target):
        pl.semaphore_signal(barrier, inc=1, device_id=target, device_id_type=MESH)

    def greet_line(k, _):
        greet(dev((y + k) % N, z, c))
        greet(dev(y, (z + k) % N, c))
        greet(dev(y, z, (c + k) % N))
        return 0

    def greet_plane(p, _):
        @pl.when(jnp.logical_or(y != c, p != c))
        def _():
            greet(dev(c, z, p))
            greet(dev(p, z, y))

        return 0

    lax.fori_loop(1, N, greet_line, 0)
    lax.fori_loop(0, N, greet_plane, 0)

    tok_in = pltpu.make_async_copy(tok_hbm, tok_ref, w_sem.at[3])
    gain_in = pltpu.make_async_copy(gain_hbm, gain_ref, w_sem.at[4])
    tok_in.start()
    gain_in.start()
    own_w1 = pltpu.make_async_copy(inw_ref.at[:, pl.ds(pl.multiple_of(z * 384, 384), 384)], w1.at[z], w_sem.at[0])
    own_w1.start()
    own_w2 = [
        pltpu.make_async_copy(outw_ref.at[:, pl.ds(384 * j, 384)], w2.at[j], w_sem.at[1 + j]) for j in range(2)
    ]
    for copy in own_w2:
        copy.start()

    tok_in.wait()
    gain_in.wait()
    values = tok_ref[...].astype(F32)
    center = jnp.mean(values, axis=1, keepdims=True)
    spread = jnp.mean(jnp.square(values - center), axis=1, keepdims=True)
    normed = ((values - center) / jnp.sqrt(spread + 1e-06) * gain_ref[...]).astype(BF16)
    for j in range(N):
        norm_out[j] = normed[:, 768 * j : 768 * (j + 1)]
    norm_in[pl.ds(y, 1)] = norm_out[pl.ds(y, 1)]

    @pl.when(y == c)
    def _():
        pl.semaphore_wait(barrier, 35)

    @pl.when(y != c)
    def _():
        pl.semaphore_wait(barrier, 37)

    def y_copy(k):
        to = (y + k) % N
        return remote(norm_out.at[to], norm_in.at[y], y_send.at[k], y_recv.at[k], dev(to, z, c))

    def w_copy(k):
        to = (z + k) % N
        return remote(
            inw_ref.at[:, pl.ds(pl.multiple_of(to * 384, 384), 384)], w1.at[z], w_send.at[k], w_recv.at[k], dev(y, to, c)
        )

    def over(start, make, act):
        def step(k, _):
            act(make(k))
            return 0

        lax.fori_loop(start, N, step, 0)

    over(1, y_copy, lambda copy: copy.start())
    for k in (1, 7, 2, 6):
        w_copy(k).start()
    over(1, y_copy, lambda copy: copy.wait_recv())
    for j in range(N):
        slab[4 * j : 4 * j + 4, 0:768] = norm_in[j].astype(F32)
    x_buf[c, z] = slab[:, 0:768].astype(BF16)

    def offset(j):
        return jnp.where(j % 2 == 1, (j + 1) // 2, -(j // 2))

    ups = 4 - core

    def xz_copy(up, s):
        at = (z - s + N) % N if up else (z + s) % N
        to = (z + 1) % N if up else (z + N - 1) % N
        return remote(x_buf.at[c, at], x_buf.at[c, at], xz_send.at[1 - up, s], xg_recv.at[c, at], dev(y, to, c))

    def x_ready(j):
        at = (z + offset(j) + N) % N

        @pl.when(j > 0)
        def _():
            remote(x_buf.at[c, at], x_buf.at[c, at], xz_send.at[0, 0], xg_recv.at[c, at], dev(y, at, c)).wait_recv()

        s = (j + 1) // 2
        for up in (1, 0):
            mine = jnp.logical_or(j == 0, j % 2 == 1 - up)

            @pl.when(jnp.logical_and(mine, s < (ups if up else 7 - ups)))
            def _():
                xz_copy(up, s).start()

    def gather_step(buf, place, send, recv, ready, i):
        def move(of, j, kind, target):
            at = (place + offset(j) + N) % N
            return remote(buf.at[of, at], buf.at[of, at], send.at[kind, j], recv.at[of, at], dev(y, z, target))

        def start(of, j, kind, target):
            move(of, j, kind, target).start()

        def arrived(of, j):
            move(of, j, 0, sibling).wait_recv()

        @pl.when(i < N)
        def _():
            ready(i)
            start(c, i, 0, right)
            start(c, i, 1, left)
            start(c, i, 2, sibling)

        @pl.when(jnp.logical_and(i >= 1, i < N + 1))
        def _():
            j = i - 1
            arrived(left, j)

            @pl.when(j % 2 == 0)
            def _():
                start(left, j, 3, right)

            start(left, j, 4, sibling)
            arrived(right, j)

            @pl.when(j % 2 == 1)
            def _():
                start(right, j, 3, left)

            start(right, j, 5, sibling)

        @pl.when(jnp.logical_and(i >= 2, i < N + 2))
        def _():
            j = i - 2
            arrived(across, j)
            start(across, j, 6, sibling)

        @pl.when(i >= 3)
        def _():
            for d in range(4):
                arrived(col_of(x + d, 1 - core), i - 3)

    def gather_sent(buf, place, send, recv):
        def step(j, _):
            for kind in range(7):
                remote(buf.at[c, j], buf.at[c, j], send.at[kind, j], recv.at[c, j], dev(y, z, sibling)).wait_send()
            return 0

        lax.fori_loop(0, N, step, 0)

    def gather_x(i, _):
        gather_step(x_buf, z, xg_send, xg_recv, x_ready, i)
        return 0

    lax.fori_loop(0, 5, gather_x, 0)
    for k in (3, 5, 4):
        w_copy(k).start()
    lax.fori_loop(5, N, gather_x, 0)
    lax.fori_loop(N, N + 3, gather_x, 0)
    own_w1.wait()
    over(1, w_copy, lambda copy: copy.wait_recv())

    def chain(q):
        h, back = q % 4, q // 4
        steps = 4 - (h + back) % 2
        return h, 1 - 2 * back, steps

    def ring_copy(at, q, s, place, neighbour):
        _, way, _ = chain(q)
        return remote(
            ring_send.at[at, q, s], ring_recv.at[at, q, s], rs_send.at[at, q, s], rs_recv.at[at, q, s],
            neighbour((place + way + N) % N),
        )

    def ring_step(at, q, s, place, neighbour, own):
        h, way, steps = chain(q)

        @pl.when(s < steps)
        def _():
            to = (place + way * (steps - s) + N) % N
            mine = own(to, h)

            @pl.when(s == 0)
            def _():
                ring_send[at, q, s] = mine.astype(BF16)

            @pl.when(s > 0)
            def _():
                before = jnp.maximum(s - 1, 0)
                ring_copy(at, q, before, place, neighbour).wait_recv()
                ring_send[at, q, s] = (mine + ring_recv[at, q, before].astype(F32)).astype(BF16)

            ring_copy(at, q, s, place, neighbour).start()

    def ring_last(at, h, place, neighbour, own):
        total = own(place, h)
        for q in (h, 4 + h):
            last = 3 - (h + q // 4) % 2
            ring_copy(at, q, last, place, neighbour).wait_recv()
            total = total + ring_recv[at, q, last].astype(F32)
        return total

    def rings(each):
        def step(i, _):
            for at, place, neighbour, own in each:
                ring_step(at, i % 8, i // 8, place, neighbour, own)
            return 0

        lax.fori_loop(0, 32, step, 0)

    def rings_sent(each):
        def step(i, _):
            for at, place, neighbour, own in each:
                q, s = i % 8, i // 8

                @pl.when(s < chain(q)[2])
                def _():
                    ring_copy(at, q, s, place, neighbour).wait_send()

            return 0

        lax.fori_loop(0, 32, step, 0)

    def along_y(to):
        return dev(to, z, c)

    def along_z(to):
        return dev(y, to, c)

    def pre_part(to, h):
        lhs = rows_of(x_buf[to, pl.ds(2 * h, 2)])
        return jnp.dot(lhs, rows_of(w1[...]), preferred_element_type=F32)

    ring_pre = (0, y, along_y, pre_part)
    rings([ring_pre])
    for h in range(4):
        hidden = gelu(ring_last(0, h, y, along_y, pre_part)).astype(BF16)
        hid_out[2 * h : 2 * h + 2] = hidden.reshape(2, 32, 384)

    def hc_copy(k):
        to = (c + k) % N
        return remote(hid_out.at[to], hid_in.at[c], hc_send.at[k], hc_recv.at[k], dev(y, z, to))

    def hy_copy(of):
        return remote(hid_in.at[of], h_buf.at[c, y], hy_send.at[of], hg_recv.at[c, y], dev(of, z, c))

    def pass_on(of):
        @pl.when(of == y)
        def _():
            h_buf[c, y] = hid_in[of]

        @pl.when(of != y)
        def _():
            hy_copy(of).start()

    over(1, hc_copy, lambda copy: copy.start())
    hid_in[pl.ds(c, 1)] = hid_out[pl.ds(c, 1)]
    pass_on(c)

    def hc_arrived(k, _):
        hc_copy(k).wait_recv()
        pass_on((c - k + N) % N)
        return 0

    lax.fori_loop(1, N, hc_arrived, 0)

    def h_ready(j):
        at = (y + offset(j) + N) % N

        @pl.when(j > 0)
        def _():
            remote(h_buf.at[c, at], h_buf.at[c, at], hy_send.at[0], hg_recv.at[c, at], dev(at, z, c)).wait_recv()

    def gather_h(i, _):
        gather_step(h_buf, y, hg_send, hg_recv, h_ready, i)
        return 0

    for copy in own_w2:
        copy.wait()
    lax.fori_loop(0, N, gather_h, 0)
    lax.fori_loop(N, N + 3, gather_h, 0)

    def out_part_a(to, h):
        return jnp.dot(rows_of(h_buf[pl.ds(2 * h, 2), to]), w2[0], preferred_element_type=F32)

    def out_part_b(to, h):
        return jnp.dot(rows_of(h_buf[to, pl.ds(2 * h, 2)]), w2[1], preferred_element_type=F32)

    ring_a, ring_b = (1, y, along_y, out_part_a), (2, z, along_z, out_part_b)
    rings([ring_a, ring_b])
    others = ((z, along_z), (y, along_y))

    def p_copy(j, k):
        place, neighbour = others[j]
        to = (place + k) % N
        return remote(part.at[j, to], part_in.at[j, place], p_send.at[j, k], p_recv.at[j, k], neighbour(to))

    for h in range(4):
        for j, (at, place, neighbour, own) in enumerate((ring_a, ring_b)):
            total = ring_last(at, h, place, neighbour, own).reshape(2, 32, 384)
            own_part[j, 2 * h : 2 * h + 2] = total
            part[j, 2 * h : 2 * h + 2] = total.astype(BF16)

    def p_start(k, _):
        for j in range(2):
            p_copy(j, k).start()
        return 0

    lax.fori_loop(1, N, p_start, 0)
    for j in range(2):
        place = others[j][0]

        def p_add(k, total):
            p_copy(j, k).wait_recv()
            return total + part_in[j, (place - k + N) % N].astype(F32)

        slab[:, 384 * j : 384 * (j + 1)] = lax.fori_loop(1, N, p_add, own_part[j, place])

    for j in range(N):
        fin_out[j] = slab[4 * j : 4 * j + 4, 0:768]

    def f_copy(p):
        return remote(fin_out.at[p], fin_in.at[c], f_send.at[p], f_recv.at[c], dev(p, z, y))

    def f_start(p, _):
        @pl.when(jnp.logical_and(y == c, p == y))
        def _():
            fin_in[c] = fin_out[p]

        @pl.when(jnp.logical_or(y != c, p != y))
        def _():
            f_copy(p).start()

        return 0

    lax.fori_loop(0, N, f_start, 0)

    over(1, y_copy, lambda copy: copy.wait_send())
    over(1, w_copy, lambda copy: copy.wait_send())
    over(1, hc_copy, lambda copy: copy.wait_send())
    gather_sent(x_buf, z, xg_send, xg_recv)
    gather_sent(h_buf, y, hg_send, hg_recv)
    for up in (1, 0):
        for s in range(4):

            @pl.when(s < (ups if up else 7 - ups))
            def _():
                xz_copy(up, s).wait_send()

    def hy_sent(of, _):
        @pl.when(of != y)
        def _():
            hy_copy(of).wait_send()

        return 0

    lax.fori_loop(0, N, hy_sent, 0)
    rings_sent([ring_pre, ring_a, ring_b])

    def p_sent(k, _):
        for j in range(2):
            p_copy(j, k).wait_send()
        return 0

    lax.fori_loop(1, N, p_sent, 0)

    def plane_sent(p, _):
        @pl.when(jnp.logical_or(y != c, p != c))
        def _():
            f_copy(p).wait_send()
            remote(fin_out.at[p], fin_in.at[p], f_send.at[p], f_recv.at[p], dev(c, z, p)).wait_recv()

        return 0

    lax.fori_loop(0, N, plane_sent, 0)
    for j in range(N):
        cols = slice(768 * j, 768 * (j + 1))
        out_ref[:, cols] = (tok_ref[:, cols].astype(F32) + fin_in[j]).astype(BF16)


def body(tokens, norm_gain, in_weight, out_weight):
    dma = pltpu.SemaphoreType.DMA
    return pl.pallas_call(
        kernel,
        out_shape=jax.ShapeDtypeStruct(tokens.shape, BF16),
        in_specs=[pl.BlockSpec(memory_space=pltpu.HBM)] * 4,
        out_specs=pl.BlockSpec(memory_space=pltpu.VMEM),
        scratch_shapes=[
            pltpu.VMEM((4, 6144), BF16),
            pltpu.VMEM((1, 6144), F32),
            pltpu.VMEM((N, 96, 384), BF16),
            pltpu.VMEM((2, 384, 384), BF16),
            pltpu.VMEM((N, 4, 768), BF16),
            pltpu.VMEM((N, 4, 768), BF16),
            pltpu.VMEM((32, 768), F32),
            pltpu.VMEM((N, N, 32, 768), BF16),
            pltpu.VMEM((N, 32, 384), BF16),
            pltpu.VMEM((N, 32, 384), BF16),
            pltpu.VMEM((N, N, 32, 384), BF16),
            pltpu.VMEM((3, 8, 4, 64, 384), BF16),
            pltpu.VMEM((3, 8, 4, 64, 384), BF16),
            pltpu.VMEM((2, N, 32, 384), BF16),
            pltpu.VMEM((2, N, 32, 384), BF16),
            pltpu.VMEM((2, N, 32, 384), F32),
            pltpu.VMEM((N, 4, 768), F32),
            pltpu.VMEM((N, 4, 768), F32),
            dma((5,)),
            dma((N,)), dma((N,)), dma((N,)), dma((N,)),
            dma((2, 4)), dma((7, N)), dma((N, N)), dma((7, N)), dma((N, N)),
            dma((N,)), dma((N,)), dma((N,)),
            dma((3, 8, 4)), dma((3, 8, 4)),
            dma((2, N)), dma((2, N)),
            dma((N,)), dma((N,)),
        ],
        compiler_params=pltpu.CompilerParams(
            collective_id=0, has_side_effects=True, vmem_limit_bytes=62 * 1024 * 1024
        ),
        cost_estimate=pl.CostEstimate(flops=2_500_000_000, bytes_accessed=1_300_000, transcendentals=100_000),
    )(tokens, norm_gain.reshape(1, -1), in_weight, out_weight)


def solution(mesh):
    return jax.shard_map(
        body,
        mesh=mesh,
        in_specs=(P(("row", "col"), None), P(), P("row", "col"), P("row", "col")),
        out_specs=P(("row", "col"), None),
        check_vma=False,
    )
```

time: 143 us -> 139 us (0.972)
  the two profiles are of different devices: /device:TPU:1 before, /device:TPU:4 now
where the time goes in v2:
time: 139 us
  Pallas kernels  138 us (99%)
  local copies, waits for them, and re-layouts  1.44 us (1%)
    pallas_call x1, Pallas kernels, body(): pl.pallas_call(kernel, out_shape=jax.ShapeDtypeStruct(tokens.shape, BF16)...  138 us

profile of v2, /device:TPU:4, one launch (start us, length us, event | category | flops | bytes accessed | tf_op | source)
XLA Modules:
  0.0 139.2 jit_solution(16559884672586653522)
XLA Ops:
  0.0 137.7 %shard_map.46 = bf16[4,6144]{1,0:T(4,128)(2,1)} custom-call(bf16[4,6144]{1,0:T(4,128)(2,1)} %tok_hbm.1, f32[1,6144]{1,0:T(1,128)} %bitcast.1, bf16[96,3072]{1,0:T(8,128)(2,1)} %inw_ref.1, bf16[384,768]{1,0:T(8,128)(2,1)} %outw_ref.1), custom_call_target="tpu_custom_call" | custom-call | flops 2500000000 | bytes 1300000 | tf_op jit(solution)/shard_map/pallas_call | solution.py:435
  137.7 1.4 %copy.6 = bf16[4,6144]{1,0:T(4,128)(2,1)} copy(bf16[4,6144]{1,0:T(4,128)(2,1)} %shard_map.46) | data formatting | bytes 98304

commit v3 on v2

--- a/solution.py
+++ b/solution.py
@@ -123,29 +123,39 @@
     def offset(j):
         return jnp.where(j % 2 == 1, (j + 1) // 2, -(j // 2))
 
-    ups = 4 - core
-
-    def xz_copy(up, s):
-        at = (z - s + N) % N if up else (z + s) % N
-        to = (z + 1) % N if up else (z + N - 1) % N
-        return remote(x_buf.at[c, at], x_buf.at[c, at], xz_send.at[1 - up, s], xg_recv.at[c, at], dev(y, to, c))
+    def xz_copy(kind, at, shift):
+        at, to = (z + at + N) % N, (z + shift + N) % N
+        return remote(x_buf.at[c, at], x_buf.at[c, at], xz_send.at[kind], xg_recv.at[c, at], dev(y, to, c))
+
+    xz_own = [xz_copy(0, 0, 2), xz_copy(1, 0, -2), xz_copy(2, 0, 1), xz_copy(3, 0, -1)]
+    xz_near = [xz_copy(4, 2, -1), xz_copy(5, -2, 1)]
+
+    def xz_far(act):
+        @pl.when(core == 0)
+        def _():
+            act(xz_copy(6, -2, 2))
+
+        @pl.when(core == 1)
+        def _():
+            act(xz_copy(6, 2, -2))
+
+    for copy in xz_own:
+        copy.start()
 
     def x_ready(j):
         at = (z + offset(j) + N) % N
 
         @pl.when(j > 0)
         def _():
-            remote(x_buf.at[c, at], x_buf.at[c, at], xz_send.at[0, 0], xg_recv.at[c, at], dev(y, at, c)).wait_recv()
-
-        s = (j + 1) // 2
-        for up in (1, 0):
-            mine = jnp.logical_or(j == 0, j % 2 == 1 - up)
-
-            @pl.when(jnp.logical_and(mine, s < (ups if up else 7 - ups)))
-            def _():
-                xz_copy(up, s).start()
-
-    def gather_step(buf, place, send, recv, ready, i):
+            remote(x_buf.at[c, at], x_buf.at[c, at], xz_send.at[0], xg_recv.at[c, at], dev(y, at, c)).wait_recv()
+
+        @pl.when(j == 4)
+        def _():
+            xz_near[0].start()
+            xz_near[1].start()
+            xz_far(lambda copy: copy.start())
+
+    def gather(buf, place, send, recv, ready, between=None):
         def move(of, j, kind, target):
             at = (place + offset(j) + N) % N
             return remote(buf.at[of, at], buf.at[of, at], send.at[kind, j], recv.at[of, at], dev(y, z, target))
@@ -156,16 +166,14 @@
         def arrived(of, j):
             move(of, j, 0, sibling).wait_recv()
 
-        @pl.when(i < N)
-        def _():
-            ready(i)
-            start(c, i, 0, right)
-            start(c, i, 1, left)
-            start(c, i, 2, sibling)
-
-        @pl.when(jnp.logical_and(i >= 1, i < N + 1))
-        def _():
-            j = i - 1
+        def own_step(j, _):
+            ready(j)
+            start(c, j, 0, right)
+            start(c, j, 1, left)
+            start(c, j, 2, sibling)
+            return 0
+
+        def near_step(j, _):
             arrived(left, j)
 
             @pl.when(j % 2 == 0)
@@ -180,17 +188,23 @@
                 start(right, j, 3, left)
 
             start(right, j, 5, sibling)
-
-        @pl.when(jnp.logical_and(i >= 2, i < N + 2))
-        def _():
-            j = i - 2
+            return 0
+
+        def far_step(j, _):
             arrived(across, j)
             start(across, j, 6, sibling)
-
-        @pl.when(i >= 3)
-        def _():
+            return 0
+
+        def rest_step(j, _):
             for d in range(4):
-                arrived(col_of(x + d, 1 - core), i - 3)
+                arrived(col_of(x + d, 1 - core), j)
+            return 0
+
+        lax.fori_loop(0, N, own_step, 0)
+        if between is not None:
+            between()
+        for step in (near_step, far_step, rest_step):
+            lax.fori_loop(0, N, step, 0)
 
     def gather_sent(buf, place, send, recv):
         def step(j, _):
@@ -200,15 +214,11 @@
 
         lax.fori_loop(0, N, step, 0)
 
-    def gather_x(i, _):
-        gather_step(x_buf, z, xg_send, xg_recv, x_ready, i)
-        return 0
-
-    lax.fori_loop(0, 5, gather_x, 0)
-    for k in (3, 5, 4):
-        w_copy(k).start()
-    lax.fori_loop(5, N, gather_x, 0)
-    lax.fori_loop(N, N + 3, gather_x, 0)
+    def rest_of_w():
+        for k in (3, 5, 4):
+            w_copy(k).start()
+
+    gather(x_buf, z, xg_send, xg_recv, x_ready, rest_of_w)
     own_w1.wait()
     over(1, w_copy, lambda copy: copy.wait_recv())
 
@@ -323,14 +333,9 @@
         def _():
             remote(h_buf.at[c, at], h_buf.at[c, at], hy_send.at[0], hg_recv.at[c, at], dev(at, z, c)).wait_recv()
 
-    def gather_h(i, _):
-        gather_step(h_buf, y, hg_send, hg_recv, h_ready, i)
-        return 0
-
     for copy in own_w2:
         copy.wait()
-    lax.fori_loop(0, N, gather_h, 0)
-    lax.fori_loop(N, N + 3, gather_h, 0)
+    gather(h_buf, y, hg_send, hg_recv, h_ready)
 
     def out_part_a(to, h):
         return jnp.dot(rows_of(h_buf[pl.ds(2 * h, 2), to]), w2[0], preferred_element_type=F32)
@@ -392,12 +397,9 @@
     over(1, hc_copy, lambda copy: copy.wait_send())
     gather_sent(x_buf, z, xg_send, xg_recv)
     gather_sent(h_buf, y, hg_send, hg_recv)
-    for up in (1, 0):
-        for s in range(4):
-
-            @pl.when(s < (ups if up else 7 - ups))
-            def _():
-                xz_copy(up, s).wait_send()
+    for copy in xz_own + xz_near:
+        copy.wait_send()
+    xz_far(lambda copy: copy.wait_send())
 
     def hy_sent(of, _):
         @pl.when(of != y)
@@ -458,7 +460,7 @@
             pltpu.VMEM((N, 4, 768), F32),
             dma((5,)),
             dma((N,)), dma((N,)), dma((N,)), dma((N,)),
-            dma((2, 4)), dma((7, N)), dma((N, N)), dma((7, N)), dma((N, N)),
+            dma((7,)), dma((7, N)), dma((N, N)), dma((7, N)), dma((N, N)),
             dma((N,)), dma((N,)), dma((N,)),
             dma((3, 8, 4)), dma((3, 8, 4)),
             dma((2, N)), dma((2, N)),

time: 139 us -> 123 us (0.88)
  the two profiles are of different devices: /device:TPU:4 before, /device:TPU:1 now
where the time goes in v3:
time: 123 us; the launch traced here: 122 us
  Pallas kernels  121 us (98%)
  local copies, waits for them, and re-layouts  1.44 us (1%)
    pallas_call x1, Pallas kernels, body(): pl.pallas_call(kernel, out_shape=jax.ShapeDtypeStruct(tokens.shape, BF16)...  121 us

profile of v3, /device:TPU:1, one launch (start us, length us, event | category | flops | bytes accessed | tf_op | source)
XLA Modules:
  0.0 122.5 jit_solution(14178925917026506014)
XLA Ops:
  0.0 121.0 %shard_map.46 = bf16[4,6144]{1,0:T(4,128)(2,1)} custom-call(bf16[4,6144]{1,0:T(4,128)(2,1)} %tok_hbm.1, f32[1,6144]{1,0:T(1,128)} %bitcast.1, bf16[96,3072]{1,0:T(8,128)(2,1)} %inw_ref.1, bf16[384,768]{1,0:T(8,128)(2,1)} %outw_ref.1), custom_call_target="tpu_custom_call" | custom-call | flops 2500000000 | bytes 1300000 | tf_op jit(solution)/shard_map/pallas_call | solution.py:437
  121.0 1.4 %copy.6 = bf16[4,6144]{1,0:T(4,128)(2,1)} copy(bf16[4,6144]{1,0:T(4,128)(2,1)} %shard_map.46) | data formatting | bytes 98304

commit v4 on v0

v4 whole, which is shorter than its diff:
```python
import jax
import jax.numpy as jnp
from jax import lax
from jax.experimental import pallas as pl
from jax.experimental.pallas import tpu as pltpu
from jax.sharding import PartitionSpec as P

MESH = pl.DeviceIdType.MESH
N = 8
BF16 = jnp.bfloat16
F32 = jnp.float32


def gelu(v):
    return 0.5 * v * (1.0 + jnp.tanh(0.7978845608028654 * (v + 0.044715 * (v * v * v))))


def rows_of(block):
    return block.reshape(-1, block.shape[-1])


S_Y, S_W, S_Z, S_X, S_H, S_R, S_HC, S_HY, S_P, S_F, SENDS = 0, 1, 2, 3, 5, 7, 10, 11, 12, 13, 14


def kernel(
    tok_hbm, gain_hbm, inw_ref, outw_ref, out_ref,
    tok_ref, gain_ref, w1, w2, norm_out, norm_in, slab, x_buf, pre_own, hid_out, hid_in, h_buf, out_own,
    ring_send, ring_recv, part, part_in, own_part, fin_out, fin_in,
    w_sem, sent, y_recv, w_recv, z_recv, x_recv, h_recv, hc_recv, hy_recv, rs_recv, p_recv, f_recv,
):
    row, c = lax.axis_index("row"), lax.axis_index("col")
    y, z = row // N, row % N
    x, core = c // 2, c % 2

    def dev(y_at, z_at, c_at):
        return (y_at * N + z_at, c_at)

    def col_of(x_at, core_at):
        return ((x_at + 8) % 4) * 2 + core_at

    right, left, across, sibling = col_of(x + 1, core), col_of(x - 1, core), col_of(x + 2, core), col_of(x, 1 - core)

    def remote(src, dst, kind, recv, target):
        return pltpu.make_async_remote_copy(
            src_ref=src, dst_ref=dst, send_sem=sent.at[kind], recv_sem=recv, device_id=target, device_id_type=MESH
        )

    def take(ref, recv):
        remote(ref, ref, S_Y, recv, dev(y, z, sibling)).wait_recv()

    def drain(ref, kind):
        remote(ref, ref, kind, f_recv, dev(y, z, sibling)).wait_send()

    def loop(start, end, act):
        def step(k, _):
            act(k)
            return 0

        lax.fori_loop(start, end, step, 0)

    tok_in = pltpu.make_async_copy(tok_hbm, tok_ref, w_sem.at[2])
    gain_in = pltpu.make_async_copy(gain_hbm, gain_ref, w_sem.at[3])
    tok_in.start()
    gain_in.start()

    barrier = pltpu.get_barrier_semaphore()

    def greet(target):
        pl.semaphore_signal(barrier, inc=1, device_id=target, device_id_type=MESH)

    def greet_line(k):
        greet(dev((y + k) % N, z, c))
        greet(dev(y, (z + k) % N, c))
        greet(dev(y, z, (c + k) % N))

    def greet_plane(p):
        @pl.when(jnp.logical_or(y != c, p != c))
        def _():
            greet(dev(c, z, p))
            greet(dev(p, z, y))

    loop(1, N, greet_line)
    loop(0, N, greet_plane)

    own_w1 = pltpu.make_async_copy(inw_ref.at[:, pl.ds(pl.multiple_of(z * 384, 384), 384)], w1.at[z], w_sem.at[0])
    own_w2 = pltpu.make_async_copy(outw_ref, w2, w_sem.at[1])
    own_w1.start()
    own_w2.start()

    tok_in.wait()
    gain_in.wait()
    values = tok_ref[...].astype(F32)
    center = jnp.mean(values, axis=1, keepdims=True)
    spread = jnp.mean(jnp.square(values - center), axis=1, keepdims=True)
    normed = ((values - center) / jnp.sqrt(spread + 1e-06) * gain_ref[...]).astype(BF16)
    for j in range(N):
        norm_out[j] = normed[:, 768 * j : 768 * (j + 1)]
    norm_in[pl.ds(y, 1)] = norm_out[pl.ds(y, 1)]

    @pl.when(y == c)
    def _():
        pl.semaphore_wait(barrier, 35)

    @pl.when(y != c)
    def _():
        pl.semaphore_wait(barrier, 37)

    def y_start(k):
        to = (y + k) % N
        remote(norm_out.at[to], norm_in.at[y], S_Y, y_recv, dev(to, z, c)).start()

    def w_start(k):
        to = (z + k) % N
        remote(
            inw_ref.at[:, pl.ds(pl.multiple_of(to * 384, 384), 384)], w1.at[z], S_W, w_recv, dev(y, to, c)
        ).start()

    loop(1, N, y_start)
    for k in (1, 7):
        w_start(k)
    take(norm_in.at[0:7], y_recv)
    for j in range(N):
        slab[4 * j : 4 * j + 4] = norm_in[j].astype(F32)
    for hf in range(2):
        x_buf[hf, c, z] = slab[16 * hf : 16 * hf + 16].astype(BF16)

    def z_copy(at, shift):
        at, to = (z + at + N) % N, (z + shift + N) % N
        return remote(x_buf.at[:, c, at], x_buf.at[:, c, at], S_Z, z_recv.at[at], dev(y, to, c))

    for shift in (2, -2, 1, -1):
        z_copy(0, shift).start()

    def x_own(hf):
        for off in (0, 2, -2, 1, -1, 3, -3, 4):
            at = (z + off + N) % N
            block = x_buf.at[hf, c, at]
            if hf == 0 and off != 0:
                take(x_buf.at[:, c, at], z_recv.at[at])
            if hf == 0 and off == -2:
                z_copy(2, -1).start()
                z_copy(-2, 1).start()

                @pl.when(core == 0)
                def _():
                    z_copy(-2, 2).start()

                @pl.when(core == 1)
                def _():
                    z_copy(2, -2).start()

                for k in (2, 6, 3, 5, 4):
                    w_start(k)
            remote(block, block, S_X + hf, x_recv.at[hf, at // 4], dev(y, z, right)).start()
            remote(block, block, S_X + hf, x_recv.at[hf, 2 + at // 4], dev(y, z, left)).start()
        remote(x_buf.at[hf, c], x_buf.at[hf, c], S_X + hf, x_recv.at[hf, 6], dev(y, z, sibling)).start()

    def h_own(hf):
        take(h_buf.at[hf, c, 0:7], hy_recv.at[hf])
        for g in range(2):
            block = h_buf.at[hf, c, 4 * g : 4 * g + 4]
            remote(block, block, S_H + hf, h_recv.at[hf, g], dev(y, z, right)).start()
            remote(block, block, S_H + hf, h_recv.at[hf, 2 + g], dev(y, z, left)).start()
        for g in range(2):
            block = h_buf.at[hf, c, 4 * g : 4 * g + 4]
            remote(block, block, S_H + hf, h_recv.at[hf, 4 + g], dev(y, z, across)).start()
        remote(h_buf.at[hf, c], h_buf.at[hf, c], S_H + hf, h_recv.at[hf, 6], dev(y, z, sibling)).start()

    class Gather:
        def __init__(self, buf, kind, recv):
            self.buf, self.kind, self.recv = buf, kind, recv

        def block(self, hf, of, g):
            return self.buf.at[hf, of, 4 * g : 4 * g + 4]

        def to_sibling(self, hf, of):
            block = self.buf.at[hf, of]
            remote(block, block, self.kind + hf, self.recv.at[hf, 6], dev(y, z, sibling)).start()

        def near(self, hf):
            if self.kind == S_X:
                for of, g, side, to, far in ((left, 0, 0, right, 4), (right, 1, 2, left, 5)):
                    block = self.block(hf, of, g)
                    take(block, self.recv.at[hf, side + g])
                    remote(block, block, self.kind + hf, self.recv.at[hf, far], dev(y, z, to)).start()
                self.beside(hf, ((left, 1, 0), (right, 0, 2)))
            else:
                self.beside(hf, ((left, 0, 0), (left, 1, 0)), left)
                self.beside(hf, ((right, 0, 2), (right, 1, 2)), right)

        def beside(self, hf, blocks, whole=None):
            for of, g, side in blocks:
                take(self.block(hf, of, g), self.recv.at[hf, side + g])
                if whole is None:
                    self.to_sibling(hf, of)
            if whole is not None:
                self.to_sibling(hf, whole)

        def far(self, hf):
            for g in range(2):
                take(self.block(hf, across, g), self.recv.at[hf, 4 + g])
            self.to_sibling(hf, across)

        def rest(self, hf):
            take(self.buf.at[hf, 0:4], self.recv.at[hf, 6])

    def ring_copy(at, q, s, i, place, neighbour):
        way = 1 - 2 * (i % 2)
        return remote(
            ring_send.at[at, q, s], ring_recv.at[at, q, s], S_R + at, rs_recv.at[at, q, s], neighbour((place + way + N) % N)
        )

    def rings(hf, s, each):
        def step(i):
            odd = (i % 2 + i // 2) % 2
            q = hf * 4 + i

            def act():
                for at, place, neighbour, own in each:
                    to = (place + (1 - 2 * (i % 2)) * (4 - odd - s) + N) % N
                    mine = own(hf, to, i // 2)
                    if s > 0:
                        take(ring_recv.at[at, q, s - 1], rs_recv.at[at, q, s - 1])
                        mine = mine + ring_recv[at, q, s - 1].astype(F32)
                    ring_send[at, q, s] = mine.astype(BF16)
                    ring_copy(at, q, s, i, place, neighbour).start()

            if s < 3:
                act()
            else:
                pl.when(odd == 0)(act)

        loop(0, 4, step)

    def ring_last(hf, p, ring):
        at, place, _, own = ring
        total = own(hf, place, p)
        for i in (2 * p, 2 * p + 1):
            q, s = hf * 4 + i, 3 - (p + i % 2) % 2
            take(ring_recv.at[at, q, s], rs_recv.at[at, q, s])
            total = total + ring_recv[at, q, s].astype(F32)
        return total.reshape(4, 16, 384)

    def along_y(to):
        return dev(to, z, c)

    def along_z(to):
        return dev(y, to, c)

    def pre_product(hf):
        def step(t):
            rows = rows_of(x_buf[hf, pl.ds(4 * t, 4)])
            sums = jnp.dot(rows, rows_of(w1[...]), preferred_element_type=F32)
            pre_own[hf, pl.ds(4 * t, 4)] = sums.reshape(4, N, 16, 384)

        loop(0, 2, step)

    def out_product(hf):
        def step(t):
            rows = rows_of(h_buf[hf, pl.ds(4 * t, 4)])
            sums = jnp.dot(rows, w2[...], preferred_element_type=F32)
            out_own[hf, pl.ds(4 * t, 4)] = sums.reshape(4, N, 16, 768)

        loop(0, 2, step)

    def pre_part(hf, to, p):
        return rows_of(pre_own[hf, to, pl.ds(4 * p, 4)])

    def out_part_a(hf, to, p):
        return rows_of(out_own[hf, pl.ds(4 * p, 4), to, :, 0:384])

    def out_part_b(hf, to, p):
        return rows_of(out_own[hf, to, pl.ds(4 * p, 4), :, 384:768])

    ring_pre = (0, y, along_y, pre_part)
    ring_out = ((1, y, along_y, out_part_a), (2, z, along_z, out_part_b))

    def pass_on(hf, of):
        @pl.when(of == y)
        def _():
            h_buf[hf, c, y] = hid_in[hf, of]

        @pl.when(of != y)
        def _():
            remote(hid_in.at[hf, of], h_buf.at[hf, c, y], S_HY, hy_recv.at[hf], dev(of, z, c)).start()

    def hidden(hf):
        for p in range(2):
            hid_out[hf, 4 * p : 4 * p + 4] = gelu(ring_last(hf, p, ring_pre)).astype(BF16)

        def start(k):
            to = (c + k) % N
            remote(hid_out.at[hf, to], hid_in.at[hf, c], S_HC, hc_recv.at[hf], dev(y, z, to)).start()

        loop(1, N, start)
        hid_in[hf, c] = hid_out[hf, c]
        pass_on(hf, c)

    def hidden_on(hf):
        take(hid_in.at[hf, 0:7], hc_recv.at[hf])
        loop(1, N, lambda k: pass_on(hf, (c + k) % N))

    others = ((z, along_z), (y, along_y))

    def rest_of_sum(hf):
        for j in range(2):
            for p in range(2):
                total = ring_last(hf, p, ring_out[j])
                own_part[j, hf, 4 * p : 4 * p + 4] = total
                part[j, hf, 4 * p : 4 * p + 4] = total.astype(BF16)

        def start(k):
            for j, (place, neighbour) in enumerate(others):
                to = (place + k) % N
                remote(part.at[j, hf, to], part_in.at[j, hf, place], S_P, p_recv.at[j, hf], neighbour(to)).start()

        loop(1, N, start)

    def finish(hf):
        for j, (place, _) in enumerate(others):
            take(part_in.at[j, hf, 0:7], p_recv.at[j, hf])
            total = own_part[j, hf, place]
            for k in range(1, N):
                total = total + part_in[j, hf, (place + k) % N].astype(F32)
            slab[16 * hf : 16 * hf + 16, 384 * j : 384 * (j + 1)] = total
        for p in range(4 * hf, 4 * hf + 4):
            fin_out[p] = slab[4 * p : 4 * p + 4]

            @pl.when(jnp.logical_and(y == c, p == y))
            def _():
                fin_in[c] = fin_out[p]

            @pl.when(jnp.logical_or(y != c, p != y))
            def _():
                remote(fin_out.at[p], fin_in.at[c], S_F, f_recv, dev(p, z, y)).start()

    gx, gh = Gather(x_buf, S_X, x_recv), Gather(h_buf, S_H, h_recv)
    x_own(0)
    gx.near(0)
    x_own(1)
    gx.far(0)
    gx.rest(0)
    own_w1.wait()
    take(w1.at[0:7], w_recv)
    pre_product(0)
    rings(0, 0, [ring_pre])
    gx.near(1)
    gx.far(1)
    rings(0, 1, [ring_pre])
    gx.rest(1)
    pre_product(1)
    rings(1, 0, [ring_pre])
    rings(0, 2, [ring_pre])
    rings(1, 1, [ring_pre])
    rings(0, 3, [ring_pre])
    rings(1, 2, [ring_pre])
    hidden(0)
    rings(1, 3, [ring_pre])
    hidden_on(0)
    hidden(1)
    own_w2.wait()
    h_own(0)
    hidden_on(1)
    gh.near(0)
    h_own(1)
    gh.far(0)
    gh.rest(0)
    out_product(0)
    rings(0, 0, ring_out)
    gh.near(1)
    rings(0, 1, ring_out)
    gh.far(1)
    gh.rest(1)
    out_product(1)
    rings(1, 0, ring_out)
    rings(0, 2, ring_out)
    rings(1, 1, ring_out)
    rings(0, 3, ring_out)
    rings(1, 2, ring_out)
    rest_of_sum(0)
    rings(1, 3, ring_out)
    finish(0)
    rest_of_sum(1)
    finish(1)

    drain(norm_out.at[0:7], S_Y)
    drain(w1.at[0:7], S_W)
    drain(x_buf.at[:, 0, 0:7], S_Z)
    for hf in range(2):
        drain(x_buf.at[hf, 0:7], S_X + hf)
        drain(h_buf.at[hf, 0:7], S_H + hf)
    for at in range(3):
        drain(ring_send.at[at, 0:7], S_R + at)
    drain(hid_out.at[:, 0:7], S_HC)
    drain(hid_in.at[:, 0:7], S_HY)
    drain(part.at[:, :, 0:7], S_P)

    @pl.when(y == c)
    def _():
        drain(fin_out.at[0:7], S_F)
        take(fin_in.at[0:7], f_recv)

    @pl.when(y != c)
    def _():
        drain(fin_out, S_F)
        take(fin_in, f_recv)

    for j in range(N):
        cols = slice(768 * j, 768 * (j + 1))
        out_ref[:, cols] = (tok_ref[:, cols].astype(F32) + fin_in[j]).astype(BF16)


def body(tokens, norm_gain, in_weight, out_weight):
    dma = pltpu.SemaphoreType.DMA
    return pl.pallas_call(
        kernel,
        out_shape=jax.ShapeDtypeStruct(tokens.shape, BF16),
        in_specs=[pl.BlockSpec(memory_space=pltpu.HBM)] * 4,
        out_specs=pl.BlockSpec(memory_space=pltpu.VMEM),
        scratch_shapes=[
            pltpu.VMEM((4, 6144), BF16),
            pltpu.VMEM((1, 6144), F32),
            pltpu.VMEM((N, 96, 384), BF16),
            pltpu.VMEM((384, 768), BF16),
            pltpu.VMEM((N, 4, 768), BF16),
            pltpu.VMEM((N, 4, 768), BF16),
            pltpu.VMEM((32, 768), F32),
            pltpu.VMEM((2, N, N, 16, 768), BF16),
            pltpu.VMEM((2, N, N, 16, 384), F32),
            pltpu.VMEM((2, N, 16, 384), BF16),
            pltpu.VMEM((2, N, 16, 384), BF16),
            pltpu.VMEM((2, N, N, 16, 384), BF16),
            pltpu.VMEM((2, N, N, 16, 768), F32),
            pltpu.VMEM((3, 8, 4, 64, 384), BF16),
            pltpu.VMEM((3, 8, 4, 64, 384), BF16),
            pltpu.VMEM((2, 2, N, 16, 384), BF16),
            pltpu.VMEM((2, 2, N, 16, 384), BF16),
            pltpu.VMEM((2, 2, N, 16, 384), F32),
            pltpu.VMEM((N, 4, 768), F32),
            pltpu.VMEM((N, 4, 768), F32),
            dma((4,)), dma((SENDS,)), dma, dma, dma((N,)), dma((2, 7)), dma((2, 7)), dma((2,)), dma((2,)),
            dma((3, 8, 4)), dma((2, 2)), dma,
        ],
        compiler_params=pltpu.CompilerParams(
            collective_id=0, has_side_effects=True, vmem_limit_bytes=62 * 1024 * 1024
        ),
        cost_estimate=pl.CostEstimate(flops=2_500_000_000, bytes_accessed=1_300_000, transcendentals=100_000),
    )(tokens, norm_gain.reshape(1, -1), in_weight, out_weight)


def solution(mesh):
    return jax.shard_map(
        body,
        mesh=mesh,
        in_specs=(P(("row", "col"), None), P(), P("row", "col"), P("row", "col")),
        out_specs=P(("row", "col"), None),
        check_vma=False,
    )
```

time: 407 us -> 115 us (0.28)
  the two profiles are of different devices: /device:TPU:32 before, /device:TPU:50 now
where the time goes in v4:
time: 115 us; the launch traced here: 114 us
  Pallas kernels  113 us (98%)
  local copies, waits for them, and re-layouts  1.44 us (1%)
    pallas_call x1, Pallas kernels, body(): pl.pallas_call(kernel, out_shape=jax.ShapeDtypeStruct(tokens.shape, BF16)...  113 us

profile of v4, /device:TPU:50, one launch (start us, length us, event | category | flops | bytes accessed | tf_op | source)
XLA Modules:
  0.0 114.1 jit_solution(617917422654181328)
XLA Ops:
  0.0 112.7 %shard_map.46 = bf16[4,6144]{1,0:T(4,128)(2,1)} custom-call(bf16[4,6144]{1,0:T(4,128)(2,1)} %tok_hbm.1, f32[1,6144]{1,0:T(1,128)} %bitcast.1, bf16[96,3072]{1,0:T(8,128)(2,1)} %inw_ref.1, bf16[384,768]{1,0:T(8,128)(2,1)} %outw_ref.1), custom_call_target="tpu_custom_call" | custom-call | flops 2500000000 | bytes 1300000 | tf_op jit(solution)/shard_map/pallas_call | solution.py:415
  112.7 1.4 %copy.6 = bf16[4,6144]{1,0:T(4,128)(2,1)} copy(bf16[4,6144]{1,0:T(4,128)(2,1)} %shard_map.46) | data formatting | bytes 98304

commit v5 on v4

--- a/solution.py
+++ b/solution.py
@@ -24,9 +24,9 @@
 
 def kernel(
     tok_hbm, gain_hbm, inw_ref, outw_ref, out_ref,
-    tok_ref, gain_ref, w1, w2, norm_out, norm_in, slab, x_buf, pre_own, hid_out, hid_in, h_buf, out_own,
+    tok_ref, gain_ref, w1, w2, norm_out, norm_in, slab, x_buf, pre_own, own_out, sum_in, hid_in, h_buf, out_own,
     ring_send, ring_recv, part, part_in, own_part, fin_out, fin_in,
-    w_sem, sent, y_recv, w_recv, z_recv, x_recv, h_recv, hc_recv, hy_recv, rs_recv, p_recv, f_recv,
+    w_sem, sent, y_recv, w_recv, z_recv, x_recv, h_recv, last_recv, own_recv, hy_recv, rs_recv, p_recv, f_recv,
 ):
     row, c = lax.axis_index("row"), lax.axis_index("col")
     y, z = row // N, row % N
@@ -78,6 +78,11 @@
         def _():
             greet(dev(c, z, p))
             greet(dev(p, z, y))
+
+        @pl.when(p != c)
+        def _():
+            greet(dev((y + 1) % N, z, p))
+            greet(dev((y + N - 1) % N, z, p))
 
     loop(1, N, greet_line)
     loop(0, N, greet_plane)
@@ -99,11 +104,11 @@
 
     @pl.when(y == c)
     def _():
-        pl.semaphore_wait(barrier, 35)
+        pl.semaphore_wait(barrier, 49)
 
     @pl.when(y != c)
     def _():
-        pl.semaphore_wait(barrier, 37)
+        pl.semaphore_wait(barrier, 51)
 
     def y_start(k):
         to = (y + k) % N
@@ -116,7 +121,7 @@
         ).start()
 
     loop(1, N, y_start)
-    for k in (1, 7):
+    for k in (1, 7, 2, 6):
         w_start(k)
     take(norm_in.at[0:7], y_recv)
     for j in range(N):
@@ -124,85 +129,80 @@
     for hf in range(2):
         x_buf[hf, c, z] = slab[16 * hf : 16 * hf + 16].astype(BF16)
 
-    def z_copy(at, shift):
+    def z_copy(hf, at, shift):
         at, to = (z + at + N) % N, (z + shift + N) % N
-        return remote(x_buf.at[:, c, at], x_buf.at[:, c, at], S_Z, z_recv.at[at], dev(y, to, c))
-
-    for shift in (2, -2, 1, -1):
-        z_copy(0, shift).start()
+        return remote(x_buf.at[hf, c, at], x_buf.at[hf, c, at], S_Z, z_recv.at[hf, at], dev(y, to, c))
+
+    for hf in range(2):
+        for shift in (2, -2, 1, -1):
+            z_copy(hf, 0, shift).start()
+
+    def z_take(hf, off):
+        at = (z + off + N) % N
+        take(x_buf.at[hf, c, at], z_recv.at[hf, at])
+
+    def z_relay(hf):
+        z_copy(hf, 2, -1).start()
+        z_copy(hf, -2, 1).start()
+
+        @pl.when(core == 0)
+        def _():
+            z_copy(hf, -2, 2).start()
+
+        @pl.when(core == 1)
+        def _():
+            z_copy(hf, 2, -2).start()
+
+    def x_send(hf, off):
+        at = (z + off + N) % N
+        block = x_buf.at[hf, c, at]
+        for side, to in enumerate((right, left, across)):
+            remote(block, block, S_X + hf, x_recv.at[hf, side], dev(y, z, to)).start()
 
     def x_own(hf):
-        for off in (0, 2, -2, 1, -1, 3, -3, 4):
-            at = (z + off + N) % N
-            block = x_buf.at[hf, c, at]
-            if hf == 0 and off != 0:
-                take(x_buf.at[:, c, at], z_recv.at[at])
-            if hf == 0 and off == -2:
-                z_copy(2, -1).start()
-                z_copy(-2, 1).start()
-
-                @pl.when(core == 0)
-                def _():
-                    z_copy(-2, 2).start()
-
-                @pl.when(core == 1)
-                def _():
-                    z_copy(2, -2).start()
-
-                for k in (2, 6, 3, 5, 4):
-                    w_start(k)
-            remote(block, block, S_X + hf, x_recv.at[hf, at // 4], dev(y, z, right)).start()
-            remote(block, block, S_X + hf, x_recv.at[hf, 2 + at // 4], dev(y, z, left)).start()
-        remote(x_buf.at[hf, c], x_buf.at[hf, c], S_X + hf, x_recv.at[hf, 6], dev(y, z, sibling)).start()
+        x_send(hf, 0)
+        if hf == 0:
+            for half in range(2):
+                z_take(half, 2)
+                z_take(half, -2)
+                z_relay(half)
+            for k in (3, 5, 4):
+                w_start(k)
+        for off in (2, -2):
+            x_send(hf, off)
+        for off in (1, -1, 3, -3, 4):
+            z_take(hf, off)
+            x_send(hf, off)
+        remote(x_buf.at[hf, c], x_buf.at[hf, c], S_X + hf, x_recv.at[hf, 3], dev(y, z, sibling)).start()
 
     def h_own(hf):
-        take(h_buf.at[hf, c, 0:7], hy_recv.at[hf])
-        for g in range(2):
-            block = h_buf.at[hf, c, 4 * g : 4 * g + 4]
-            remote(block, block, S_H + hf, h_recv.at[hf, g], dev(y, z, right)).start()
-            remote(block, block, S_H + hf, h_recv.at[hf, 2 + g], dev(y, z, left)).start()
-        for g in range(2):
-            block = h_buf.at[hf, c, 4 * g : 4 * g + 4]
-            remote(block, block, S_H + hf, h_recv.at[hf, 4 + g], dev(y, z, across)).start()
-        remote(h_buf.at[hf, c], h_buf.at[hf, c], S_H + hf, h_recv.at[hf, 6], dev(y, z, sibling)).start()
+        for off in (0, 1, -1, 2, -2, 3, -3, 4):
+            at = (y + off + N) % N
+            block = h_buf.at[hf, c, at]
+            if off != 0:
+                take(block, hy_recv.at[hf, at])
+            for side, to in enumerate((right, left, across)):
+                remote(block, block, S_H + hf, h_recv.at[hf, side], dev(y, z, to)).start()
+        remote(h_buf.at[hf, c], h_buf.at[hf, c], S_H + hf, h_recv.at[hf, 3], dev(y, z, sibling)).start()
 
     class Gather:
         def __init__(self, buf, kind, recv):
             self.buf, self.kind, self.recv = buf, kind, recv
 
-        def block(self, hf, of, g):
-            return self.buf.at[hf, of, 4 * g : 4 * g + 4]
-
-        def to_sibling(self, hf, of):
-            block = self.buf.at[hf, of]
-            remote(block, block, self.kind + hf, self.recv.at[hf, 6], dev(y, z, sibling)).start()
+        def to_sibling(self, hf, side):
+            block = self.buf.at[hf, (left, right, across)[side]]
+            take(block, self.recv.at[hf, side])
+            remote(block, block, self.kind + hf, self.recv.at[hf, 3], dev(y, z, sibling)).start()
 
         def near(self, hf):
-            if self.kind == S_X:
-                for of, g, side, to, far in ((left, 0, 0, right, 4), (right, 1, 2, left, 5)):
-                    block = self.block(hf, of, g)
-                    take(block, self.recv.at[hf, side + g])
-                    remote(block, block, self.kind + hf, self.recv.at[hf, far], dev(y, z, to)).start()
-                self.beside(hf, ((left, 1, 0), (right, 0, 2)))
-            else:
-                self.beside(hf, ((left, 0, 0), (left, 1, 0)), left)
-                self.beside(hf, ((right, 0, 2), (right, 1, 2)), right)
-
-        def beside(self, hf, blocks, whole=None):
-            for of, g, side in blocks:
-                take(self.block(hf, of, g), self.recv.at[hf, side + g])
-                if whole is None:
-                    self.to_sibling(hf, of)
-            if whole is not None:
-                self.to_sibling(hf, whole)
+            self.to_sibling(hf, 0)
+            self.to_sibling(hf, 1)
 
         def far(self, hf):
-            for g in range(2):
-                take(self.block(hf, across, g), self.recv.at[hf, 4 + g])
-            self.to_sibling(hf, across)
+            self.to_sibling(hf, 2)
 
         def rest(self, hf):
-            take(self.buf.at[hf, 0:4], self.recv.at[hf, 6])
+            take(self.buf.at[hf, 0:4], self.recv.at[hf, 3])
 
     def ring_copy(at, q, s, i, place, neighbour):
         way = 1 - 2 * (i % 2)
@@ -223,7 +223,13 @@
                         take(ring_recv.at[at, q, s - 1], rs_recv.at[at, q, s - 1])
                         mine = mine + ring_recv[at, q, s - 1].astype(F32)
                     ring_send[at, q, s] = mine.astype(BF16)
-                    ring_copy(at, q, s, i, place, neighbour).start()
+                    if at > 0 or s < 2:
+                        ring_copy(at, q, s, i, place, neighbour).start()
+                    elif s == 2:
+                        pl.when(odd == 0)(lambda: ring_copy(at, q, s, i, place, neighbour).start())
+                        pl.when(odd == 1)(lambda: scatter(hf, q, s, i))
+                    else:
+                        scatter(hf, q, s, i)
 
             if s < 3:
                 act()
@@ -231,6 +237,24 @@
                 pl.when(odd == 0)(act)
 
         loop(0, 4, step)
+
+    def scatter(hf, q, s, i):
+        to = (y + 1 - 2 * (i % 2) + N) % N
+        for j in range(4):
+            remote(
+                ring_send.at[0, q, s, 16 * j : 16 * j + 16], sum_in.at[hf, i % 2, c], S_R, last_recv.at[hf],
+                dev(to, z, i // 2 * 4 + j),
+            ).start()
+
+    def scatter_own(hf):
+        own_out[hf] = pre_own[hf, y].astype(BF16)
+
+        def start(k):
+            to = (c + k) % N
+            remote(own_out.at[hf, to], sum_in.at[hf, 2, c], S_HC, own_recv.at[hf], dev(y, z, to)).start()
+
+        loop(1, N, start)
+        sum_in[hf, 2, c] = own_out[hf, c]
 
     def ring_last(hf, p, ring):
         at, place, _, own = ring
@@ -282,23 +306,14 @@
 
         @pl.when(of != y)
         def _():
-            remote(hid_in.at[hf, of], h_buf.at[hf, c, y], S_HY, hy_recv.at[hf], dev(of, z, c)).start()
+            remote(hid_in.at[hf, of], h_buf.at[hf, c, y], S_HY, hy_recv.at[hf, y], dev(of, z, c)).start()
 
     def hidden(hf):
-        for p in range(2):
-            hid_out[hf, 4 * p : 4 * p + 4] = gelu(ring_last(hf, p, ring_pre)).astype(BF16)
-
-        def start(k):
-            to = (c + k) % N
-            remote(hid_out.at[hf, to], hid_in.at[hf, c], S_HC, hc_recv.at[hf], dev(y, z, to)).start()
-
-        loop(1, N, start)
-        hid_in[hf, c] = hid_out[hf, c]
-        pass_on(hf, c)
-
-    def hidden_on(hf):
-        take(hid_in.at[hf, 0:7], hc_recv.at[hf])
-        loop(1, N, lambda k: pass_on(hf, (c + k) % N))
+        take(sum_in.at[hf, 0:2], last_recv.at[hf])
+        take(sum_in.at[hf, 2, 0:7], own_recv.at[hf])
+        total = sum_in[hf, 0].astype(F32) + sum_in[hf, 1].astype(F32) + sum_in[hf, 2].astype(F32)
+        hid_in[hf] = gelu(total).astype(BF16)
+        loop(0, N, lambda of: pass_on(hf, of))
 
     others = ((z, along_z), (y, along_y))
 
@@ -324,7 +339,7 @@
                 total = total + part_in[j, hf, (place + k) % N].astype(F32)
             slab[16 * hf : 16 * hf + 16, 384 * j : 384 * (j + 1)] = total
         for p in range(4 * hf, 4 * hf + 4):
-            fin_out[p] = slab[4 * p : 4 * p + 4]
+            fin_out[p] = slab[4 * p : 4 * p + 4].astype(BF16)
 
             @pl.when(jnp.logical_and(y == c, p == y))
             def _():
@@ -336,8 +351,8 @@
 
     gx, gh = Gather(x_buf, S_X, x_recv), Gather(h_buf, S_H, h_recv)
     x_own(0)
+    x_own(1)
     gx.near(0)
-    x_own(1)
     gx.far(0)
     gx.rest(0)
     own_w1.wait()
@@ -347,29 +362,29 @@
     gx.near(1)
     gx.far(1)
     rings(0, 1, [ring_pre])
+    scatter_own(0)
     gx.rest(1)
     pre_product(1)
     rings(1, 0, [ring_pre])
     rings(0, 2, [ring_pre])
     rings(1, 1, [ring_pre])
+    scatter_own(1)
     rings(0, 3, [ring_pre])
     rings(1, 2, [ring_pre])
     hidden(0)
     rings(1, 3, [ring_pre])
-    hidden_on(0)
     hidden(1)
     own_w2.wait()
     h_own(0)
-    hidden_on(1)
+    h_own(1)
     gh.near(0)
-    h_own(1)
     gh.far(0)
     gh.rest(0)
     out_product(0)
     rings(0, 0, ring_out)
     gh.near(1)
+    gh.far(1)
     rings(0, 1, ring_out)
-    gh.far(1)
     gh.rest(1)
     out_product(1)
     rings(1, 0, ring_out)
@@ -391,7 +406,7 @@
         drain(h_buf.at[hf, 0:7], S_H + hf)
     for at in range(3):
         drain(ring_send.at[at, 0:7], S_R + at)
-    drain(hid_out.at[:, 0:7], S_HC)
+    drain(own_out.at[:, 0:7], S_HC)
     drain(hid_in.at[:, 0:7], S_HY)
     drain(part.at[:, :, 0:7], S_P)
 
@@ -407,7 +422,7 @@
 
     for j in range(N):
         cols = slice(768 * j, 768 * (j + 1))
-        out_ref[:, cols] = (tok_ref[:, cols].astype(F32) + fin_in[j]).astype(BF16)
+        out_ref[:, cols] = (tok_ref[:, cols].astype(F32) + fin_in[j].astype(F32)).astype(BF16)
 
 
 def body(tokens, norm_gain, in_weight, out_weight):
@@ -428,6 +443,7 @@
             pltpu.VMEM((2, N, N, 16, 768), BF16),
             pltpu.VMEM((2, N, N, 16, 384), F32),
             pltpu.VMEM((2, N, 16, 384), BF16),
+            pltpu.VMEM((2, 3, N, 16, 384), BF16),
             pltpu.VMEM((2, N, 16, 384), BF16),
             pltpu.VMEM((2, N, N, 16, 384), BF16),
             pltpu.VMEM((2, N, N, 16, 768), F32),
@@ -436,9 +452,9 @@
             pltpu.VMEM((2, 2, N, 16, 384), BF16),
             pltpu.VMEM((2, 2, N, 16, 384), BF16),
             pltpu.VMEM((2, 2, N, 16, 384), F32),
-            pltpu.VMEM((N, 4, 768), F32),
-            pltpu.VMEM((N, 4, 768), F32),
-            dma((4,)), dma((SENDS,)), dma, dma, dma((N,)), dma((2, 7)), dma((2, 7)), dma((2,)), dma((2,)),
+            pltpu.VMEM((N, 4, 768), BF16),
+            pltpu.VMEM((N, 4, 768), BF16),
+            dma((4,)), dma((SENDS,)), dma, dma, dma((2, N)), dma((2, 4)), dma((2, 4)), dma((2,)), dma((2,)), dma((2, N)),
             dma((3, 8, 4)), dma((2, 2)), dma,
         ],
         compiler_params=pltpu.CompilerParams(

time: 115 us -> 110 us (0.957)
  Pallas kernels: 113 us -> 108 us
    pallas_call x1, Pallas kernels: 113 us -> 108 us  [body(): pl.pallas_call(kernel, out_shape=jax.ShapeDtypeStruct(tokens.shape, BF16)...]
where the time goes in v5:
time: 110 us; the launch traced here: 109 us
  Pallas kernels  108 us (98%)
  local copies, waits for them, and re-layouts  1.44 us (1%)
    pallas_call x1, Pallas kernels, body(): pl.pallas_call(kernel, out_shape=jax.ShapeDtypeStruct(tokens.shape, BF16)...  108 us

profile of v5, /device:TPU:50, one launch (start us, length us, event | category | flops | bytes accessed | tf_op | source)
XLA Modules:
  0.0 109.4 jit_solution(833641679916298452)
XLA Ops:
  0.0 107.9 %shard_map.46 = bf16[4,6144]{1,0:T(4,128)(2,1)} custom-call(bf16[4,6144]{1,0:T(4,128)(2,1)} %tok_hbm.1, f32[1,6144]{1,0:T(1,128)} %bitcast.1, bf16[96,3072]{1,0:T(8,128)(2,1)} %inw_ref.1, bf16[384,768]{1,0:T(8,128)(2,1)} %outw_ref.1), custom_call_target="tpu_custom_call" | custom-call | flops 2500000000 | bytes 1300000 | tf_op jit(solution)/shard_map/pallas_call | solution.py:430
  107.9 1.4 %copy.6 = bf16[4,6144]{1,0:T(4,128)(2,1)} copy(bf16[4,6144]{1,0:T(4,128)(2,1)} %shard_map.46) | data formatting | bytes 98304

commit v6 on v5

--- a/solution.py
+++ b/solution.py
@@ -88,9 +88,12 @@
     loop(0, N, greet_plane)
 
     own_w1 = pltpu.make_async_copy(inw_ref.at[:, pl.ds(pl.multiple_of(z * 384, 384), 384)], w1.at[z], w_sem.at[0])
-    own_w2 = pltpu.make_async_copy(outw_ref, w2, w_sem.at[1])
+    own_w2 = [
+        pltpu.make_async_copy(outw_ref.at[:, 384 * j : 384 * j + 384], w2.at[j], w_sem.at[(1, 4)[j]]) for j in range(2)
+    ]
     own_w1.start()
-    own_w2.start()
+    for copy in own_w2:
+        copy.start()
 
     tok_in.wait()
     gain_in.wait()
@@ -271,30 +274,31 @@
     def along_z(to):
         return dev(y, to, c)
 
-    def pre_product(hf):
-        def step(t):
-            rows = rows_of(x_buf[hf, pl.ds(4 * t, 4)])
-            sums = jnp.dot(rows, rows_of(w1[...]), preferred_element_type=F32)
-            pre_own[hf, pl.ds(4 * t, 4)] = sums.reshape(4, N, 16, 384)
-
-        loop(0, 2, step)
-
-    def out_product(hf):
-        def step(t):
-            rows = rows_of(h_buf[hf, pl.ds(4 * t, 4)])
-            sums = jnp.dot(rows, w2[...], preferred_element_type=F32)
-            out_own[hf, pl.ds(4 * t, 4)] = sums.reshape(4, N, 16, 768)
-
-        loop(0, 2, step)
+    FIRST, LATER = (4, 3, 5), (2, 6, 1, 7, 0)
+
+    def pre_product(hf, offsets):
+        for off in offsets:
+            at = (y + off) % N
+            sums = jnp.dot(rows_of(x_buf[hf, at]), rows_of(w1[...]), preferred_element_type=F32)
+            pre_own[hf, at] = sums.reshape(N, 16, 384)
+
+    def out_product(hf, offsets):
+        for off in offsets:
+            at = (y + off) % N
+            sums = jnp.dot(rows_of(h_buf[hf, :, at]), w2[0], preferred_element_type=F32)
+            out_own[0, hf, at] = sums.reshape(N, 16, 384)
+            at = (z + off) % N
+            sums = jnp.dot(rows_of(h_buf[hf, at]), w2[1], preferred_element_type=F32)
+            out_own[1, hf, at] = sums.reshape(N, 16, 384)
 
     def pre_part(hf, to, p):
         return rows_of(pre_own[hf, to, pl.ds(4 * p, 4)])
 
     def out_part_a(hf, to, p):
-        return rows_of(out_own[hf, pl.ds(4 * p, 4), to, :, 0:384])
+        return rows_of(out_own[0, hf, to, pl.ds(4 * p, 4)])
 
     def out_part_b(hf, to, p):
-        return rows_of(out_own[hf, to, pl.ds(4 * p, 4), :, 384:768])
+        return rows_of(out_own[1, hf, to, pl.ds(4 * p, 4)])
 
     ring_pre = (0, y, along_y, pre_part)
     ring_out = ((1, y, along_y, out_part_a), (2, z, along_z, out_part_b))
@@ -357,15 +361,17 @@
     gx.rest(0)
     own_w1.wait()
     take(w1.at[0:7], w_recv)
-    pre_product(0)
+    pre_product(0, FIRST)
     rings(0, 0, [ring_pre])
+    pre_product(0, LATER)
     gx.near(1)
     gx.far(1)
     rings(0, 1, [ring_pre])
     scatter_own(0)
     gx.rest(1)
-    pre_product(1)
+    pre_product(1, FIRST)
     rings(1, 0, [ring_pre])
+    pre_product(1, LATER)
     rings(0, 2, [ring_pre])
     rings(1, 1, [ring_pre])
     scatter_own(1)
@@ -374,20 +380,23 @@
     hidden(0)
     rings(1, 3, [ring_pre])
     hidden(1)
-    own_w2.wait()
+    for copy in own_w2:
+        copy.wait()
     h_own(0)
     h_own(1)
     gh.near(0)
     gh.far(0)
     gh.rest(0)
-    out_product(0)
+    out_product(0, FIRST)
     rings(0, 0, ring_out)
+    out_product(0, LATER)
     gh.near(1)
     gh.far(1)
     rings(0, 1, ring_out)
     gh.rest(1)
-    out_product(1)
+    out_product(1, FIRST)
     rings(1, 0, ring_out)
+    out_product(1, LATER)
     rings(0, 2, ring_out)
     rings(1, 1, ring_out)
     rings(0, 3, ring_out)
@@ -436,7 +445,7 @@
             pltpu.VMEM((4, 6144), BF16),
             pltpu.VMEM((1, 6144), F32),
             pltpu.VMEM((N, 96, 384), BF16),
-            pltpu.VMEM((384, 768), BF16),
+            pltpu.VMEM((2, 384, 384), BF16),
             pltpu.VMEM((N, 4, 768), BF16),
             pltpu.VMEM((N, 4, 768), BF16),
             pltpu.VMEM((32, 768), F32),
@@ -446,7 +455,7 @@
             pltpu.VMEM((2, 3, N, 16, 384), BF16),
             pltpu.VMEM((2, N, 16, 384), BF16),
             pltpu.VMEM((2, N, N, 16, 384), BF16),
-            pltpu.VMEM((2, N, N, 16, 768), F32),
+            pltpu.VMEM((2, 2, N, N, 16, 384), F32),
             pltpu.VMEM((3, 8, 4, 64, 384), BF16),
             pltpu.VMEM((3, 8, 4, 64, 384), BF16),
             pltpu.VMEM((2, 2, N, 16, 384), BF16),
@@ -454,7 +463,7 @@
             pltpu.VMEM((2, 2, N, 16, 384), F32),
             pltpu.VMEM((N, 4, 768), BF16),
             pltpu.VMEM((N, 4, 768), BF16),
-            dma((4,)), dma((SENDS,)), dma, dma, dma((2, N)), dma((2, 4)), dma((2, 4)), dma((2,)), dma((2,)), dma((2, N)),
+            dma((5,)), dma((SENDS,)), dma, dma, dma((2, N)), dma((2, 4)), dma((2, 4)), dma((2,)), dma((2,)), dma((2, N)),
             dma((3, 8, 4)), dma((2, 2)), dma,
         ],
         compiler_params=pltpu.CompilerParams(

time: 110 us -> 107 us (0.973)
  the two profiles are of different devices: /device:TPU:50 before, /device:TPU:59 now
where the time goes in v6:
time: 107 us
  Pallas kernels  106 us (99%)
  local copies, waits for them, and re-layouts  1.44 us (1%)
    pallas_call x1, Pallas kernels, body(): pl.pallas_call(kernel, out_shape=jax.ShapeDtypeStruct(tokens.shape, BF16)...  106 us

profile of v6, /device:TPU:59, one launch (start us, length us, event | category | flops | bytes accessed | tf_op | source)
XLA Modules:
  0.0 107.1 jit_solution(14291683084018679123)
XLA Ops:
  0.0 105.6 %shard_map.46 = bf16[4,6144]{1,0:T(4,128)(2,1)} custom-call(bf16[4,6144]{1,0:T(4,128)(2,1)} %tok_hbm.1, f32[1,6144]{1,0:T(1,128)} %bitcast.1, bf16[96,3072]{1,0:T(8,128)(2,1)} %inw_ref.1, bf16[384,768]{1,0:T(8,128)(2,1)} %outw_ref.1), custom_call_target="tpu_custom_call" | custom-call | flops 2500000000 | bytes 1300000 | tf_op jit(solution)/shard_map/pallas_call | solution.py:439
  105.6 1.4 %copy.6 = bf16[4,6144]{1,0:T(4,128)(2,1)} copy(bf16[4,6144]{1,0:T(4,128)(2,1)} %shard_map.46) | data formatting | bytes 98304

commit v7 on v6

--- a/solution.py
+++ b/solution.py
@@ -165,21 +165,26 @@
     def x_own(hf):
         x_send(hf, 0)
         if hf == 0:
-            for half in range(2):
-                z_take(half, 2)
-                z_take(half, -2)
-                z_relay(half)
-            for k in (3, 5, 4):
-                w_start(k)
+            z_take(0, 2)
+            z_take(0, -2)
+            z_relay(0)
         for off in (2, -2):
             x_send(hf, off)
         for off in (1, -1, 3, -3, 4):
             z_take(hf, off)
             x_send(hf, off)
+            if hf == 0 and off == -1:
+                z_take(1, 2)
+                z_take(1, -2)
+                z_relay(1)
+                for k in (3, 5, 4):
+                    w_start(k)
         remote(x_buf.at[hf, c], x_buf.at[hf, c], S_X + hf, x_recv.at[hf, 3], dev(y, z, sibling)).start()
 
-    def h_own(hf):
+    def h_own(hf, between=None):
         for off in (0, 1, -1, 2, -2, 3, -3, 4):
+            if off == 3 and between is not None:
+                between()
             at = (y + off + N) % N
             block = h_buf.at[hf, c, at]
             if off != 0:
@@ -379,13 +384,15 @@
     rings(1, 2, [ring_pre])
     hidden(0)
     rings(1, 3, [ring_pre])
-    hidden(1)
     for copy in own_w2:
         copy.wait()
     h_own(0)
-    h_own(1)
-    gh.near(0)
-    gh.far(0)
+    hidden(1)
+    def pass_half_0():
+        gh.near(0)
+        gh.far(0)
+
+    h_own(1, pass_half_0)
     gh.rest(0)
     out_product(0, FIRST)
     rings(0, 0, ring_out)
@@ -403,8 +410,8 @@
     rings(1, 2, ring_out)
     rest_of_sum(0)
     rings(1, 3, ring_out)
+    rest_of_sum(1)
     finish(0)
-    rest_of_sum(1)
     finish(1)
 
     drain(norm_out.at[0:7], S_Y)

time: 107 us -> 104 us (0.972)
  the two profiles are of different devices: /device:TPU:59 before, /device:TPU:50 now
where the time goes in v7:
time: 104 us
  Pallas kernels  102 us (98%)
  local copies, waits for them, and re-layouts  1.44 us (1%)
    pallas_call x1, Pallas kernels, body(): pl.pallas_call(kernel, out_shape=jax.ShapeDtypeStruct(tokens.shape, BF16)...  102 us

profile of v7, /device:TPU:50, one launch (start us, length us, event | category | flops | bytes accessed | tf_op | source)
XLA Modules:
  0.0 103.6 jit_solution(10952844325328202959)
XLA Ops:
  0.0 102.2 %shard_map.46 = bf16[4,6144]{1,0:T(4,128)(2,1)} custom-call(bf16[4,6144]{1,0:T(4,128)(2,1)} %tok_hbm.1, f32[1,6144]{1,0:T(1,128)} %bitcast.1, bf16[96,3072]{1,0:T(8,128)(2,1)} %inw_ref.1, bf16[384,768]{1,0:T(8,128)(2,1)} %outw_ref.1), custom_call_target="tpu_custom_call" | custom-call | flops 2500000000 | bytes 1300000 | tf_op jit(solution)/shard_map/pallas_call | solution.py:446
  102.2 1.4 %copy.6 = bf16[4,6144]{1,0:T(4,128)(2,1)} copy(bf16[4,6144]{1,0:T(4,128)(2,1)} %shard_map.46) | data formatting | bytes 98304

commit v8 on v7

--- a/solution.py
+++ b/solution.py
@@ -51,6 +51,9 @@
     def drain(ref, kind):
         remote(ref, ref, kind, f_recv, dev(y, z, sibling)).wait_send()
 
+    def far_first(k):
+        return 4 + (k // 2) * (2 * (k % 2) - 1)
+
     def loop(start, end, act):
         def step(k, _):
             act(k)
@@ -123,7 +126,7 @@
             inw_ref.at[:, pl.ds(pl.multiple_of(to * 384, 384), 384)], w1.at[z], S_W, w_recv, dev(y, to, c)
         ).start()
 
-    loop(1, N, y_start)
+    loop(1, N, lambda k: y_start(far_first(k)))
     for k in (1, 7, 2, 6):
         w_start(k)
     take(norm_in.at[0:7], y_recv)
@@ -159,7 +162,7 @@
     def x_send(hf, off):
         at = (z + off + N) % N
         block = x_buf.at[hf, c, at]
-        for side, to in enumerate((right, left, across)):
+        for side, to in ((2, across), (0, right), (1, left)):
             remote(block, block, S_X + hf, x_recv.at[hf, side], dev(y, z, to)).start()
 
     def x_own(hf):
@@ -189,7 +192,7 @@
             block = h_buf.at[hf, c, at]
             if off != 0:
                 take(block, hy_recv.at[hf, at])
-            for side, to in enumerate((right, left, across)):
+            for side, to in ((2, across), (0, right), (1, left)):
                 remote(block, block, S_H + hf, h_recv.at[hf, side], dev(y, z, to)).start()
         remote(h_buf.at[hf, c], h_buf.at[hf, c], S_H + hf, h_recv.at[hf, 3], dev(y, z, sibling)).start()
 
@@ -309,36 +312,33 @@
     ring_out = ((1, y, along_y, out_part_a), (2, z, along_z, out_part_b))
 
     def pass_on(hf, of):
-        @pl.when(of == y)
-        def _():
-            h_buf[hf, c, y] = hid_in[hf, of]
-
-        @pl.when(of != y)
-        def _():
-            remote(hid_in.at[hf, of], h_buf.at[hf, c, y], S_HY, hy_recv.at[hf, y], dev(of, z, c)).start()
+        remote(hid_in.at[hf, of], h_buf.at[hf, c, y], S_HY, hy_recv.at[hf, y], dev(of, z, c)).start()
 
     def hidden(hf):
         take(sum_in.at[hf, 0:2], last_recv.at[hf])
         take(sum_in.at[hf, 2, 0:7], own_recv.at[hf])
         total = sum_in[hf, 0].astype(F32) + sum_in[hf, 1].astype(F32) + sum_in[hf, 2].astype(F32)
         hid_in[hf] = gelu(total).astype(BF16)
-        loop(0, N, lambda of: pass_on(hf, of))
+        loop(1, N, lambda k: pass_on(hf, (y + far_first(k)) % N))
+        h_buf[hf, c, y] = hid_in[hf, y]
 
     others = ((z, along_z), (y, along_y))
 
     def rest_of_sum(hf):
-        for j in range(2):
-            for p in range(2):
+        def send(j, to):
+            place, neighbour = others[j]
+
+            @pl.when(to != place)
+            def _():
+                remote(part.at[j, hf, to], part_in.at[j, hf, place], S_P, p_recv.at[j, hf], neighbour(to)).start()
+
+        for p in range(2):
+            for j in range(2):
                 total = ring_last(hf, p, ring_out[j])
                 own_part[j, hf, 4 * p : 4 * p + 4] = total
                 part[j, hf, 4 * p : 4 * p + 4] = total.astype(BF16)
-
-        def start(k):
-            for j, (place, neighbour) in enumerate(others):
-                to = (place + k) % N
-                remote(part.at[j, hf, to], part_in.at[j, hf, place], S_P, p_recv.at[j, hf], neighbour(to)).start()
-
-        loop(1, N, start)
+                for to in range(4 * p, 4 * p + 4):
+                    send(j, to)
 
     def finish(hf):
         for j, (place, _) in enumerate(others):

time: 104 us -> 102 us (0.981)
  Pallas kernels: 102 us -> 100 us
    pallas_call x1, Pallas kernels: 102 us -> 100 us  [body(): pl.pallas_call(kernel, out_shape=jax.ShapeDtypeStruct(tokens.shape, BF16)...]
where the time goes in v8:
time: 102 us
  Pallas kernels  100 us (98%)
  local copies, waits for them, and re-layouts  1.44 us (1%)
    pallas_call x1, Pallas kernels, body(): pl.pallas_call(kernel, out_shape=jax.ShapeDtypeStruct(tokens.shape, BF16)...  100 us

profile of v8, /device:TPU:50, one launch (start us, length us, event | category | flops | bytes accessed | tf_op | source)
XLA Modules:
  0.0 101.6 jit_solution(12114699934589696199)
XLA Ops:
  0.0 100.1 %shard_map.46 = bf16[4,6144]{1,0:T(4,128)(2,1)} custom-call(bf16[4,6144]{1,0:T(4,128)(2,1)} %tok_hbm.1, f32[1,6144]{1,0:T(1,128)} %bitcast.1, bf16[96,3072]{1,0:T(8,128)(2,1)} %inw_ref.1, bf16[384,768]{1,0:T(8,128)(2,1)} %outw_ref.1), custom_call_target="tpu_custom_call" | custom-call | flops 2500000000 | bytes 1300000 | tf_op jit(solution)/shard_map/pallas_call | solution.py:446
  100.1 1.4 %copy.6 = bf16[4,6144]{1,0:T(4,128)(2,1)} copy(bf16[4,6144]{1,0:T(4,128)(2,1)} %shard_map.46) | data formatting | bytes 98304

commit v9 on v8

--- a/solution.py
+++ b/solution.py
@@ -76,19 +76,7 @@
         greet(dev(y, (z + k) % N, c))
         greet(dev(y, z, (c + k) % N))
 
-    def greet_plane(p):
-        @pl.when(jnp.logical_or(y != c, p != c))
-        def _():
-            greet(dev(c, z, p))
-            greet(dev(p, z, y))
-
-        @pl.when(p != c)
-        def _():
-            greet(dev((y + 1) % N, z, p))
-            greet(dev((y + N - 1) % N, z, p))
-
     loop(1, N, greet_line)
-    loop(0, N, greet_plane)
 
     own_w1 = pltpu.make_async_copy(inw_ref.at[:, pl.ds(pl.multiple_of(z * 384, 384), 384)], w1.at[z], w_sem.at[0])
     own_w2 = [
@@ -108,13 +96,7 @@
         norm_out[j] = normed[:, 768 * j : 768 * (j + 1)]
     norm_in[pl.ds(y, 1)] = norm_out[pl.ds(y, 1)]
 
-    @pl.when(y == c)
-    def _():
-        pl.semaphore_wait(barrier, 49)
-
-    @pl.when(y != c)
-    def _():
-        pl.semaphore_wait(barrier, 51)
+    pl.semaphore_wait(barrier, 21)
 
     def y_start(k):
         to = (y + k) % N

time: 102 us -> 102 us (level)
  the two profiles are of different devices: /device:TPU:50 before, /device:TPU:62 now
where the time goes in v9:
time: 102 us
  Pallas kernels  100 us (98%)
  local copies, waits for them, and re-layouts  1.44 us (1%)
    pallas_call x1, Pallas kernels, body(): pl.pallas_call(kernel, out_shape=jax.ShapeDtypeStruct(tokens.shape, BF16)...  100 us

profile of v9, /device:TPU:62, one launch (start us, length us, event | category | flops | bytes accessed | tf_op | source)
XLA Modules:
  0.0 101.5 jit_solution(8977688000335431378)
XLA Ops:
  0.0 100.1 %shard_map.46 = bf16[4,6144]{1,0:T(4,128)(2,1)} custom-call(bf16[4,6144]{1,0:T(4,128)(2,1)} %tok_hbm.1, f32[1,6144]{1,0:T(1,128)} %bitcast.1, bf16[96,3072]{1,0:T(8,128)(2,1)} %inw_ref.1, bf16[384,768]{1,0:T(8,128)(2,1)} %outw_ref.1), custom_call_target="tpu_custom_call" | custom-call | flops 2500000000 | bytes 1300000 | tf_op jit(solution)/shard_map/pallas_call | solution.py:428
  100.1 1.4 %copy.6 = bf16[4,6144]{1,0:T(4,128)(2,1)} copy(bf16[4,6144]{1,0:T(4,128)(2,1)} %shard_map.46) | data formatting | bytes 98304
